TPU v7x, 32 devices: a whole 2x2x4 slice. The times are simulated.
32 devices in a mesh: dp: 4 (over x, core), fsdp: 8 (over z, y).
Axes of the slice: x: 2, y: 2, z: 4, core: 2. Of those that a mesh axis runs over, the one named last changes fastest.
Arguments:
- tokens: bfloat16 [32, 512, 768], P(('dp', 'fsdp')), may hold values from -6 to 6
- lengths: int32 [32], P(('dp', 'fsdp')), may hold values from 8 to 512, as said below
- weight_shards: bfloat16 [7088640], P(('dp', 'fsdp')), may hold values from -1.6 to 1.6
- hidden_cotangent: bfloat16 [32, 512, 768], P(('dp', 'fsdp')), may hold values from -6 to 6
- nested_cotangent: float32 [32, 1728], P(('dp', 'fsdp')), may hold values from -6 to 6
Outputs:
- hidden_states: bfloat16 [32, 512, 768], P(('dp', 'fsdp'))
- nested_embedding: float32 [32, 1728], P(('dp', 'fsdp'))
- input_grad: float32 [32, 512, 768], P(('dp', 'fsdp'))
- weight_grad: float32 [7088640], P(('dp', 'fsdp'))
Inputs may be any that keep to these rules, and one draw needn't show every extreme that they name: lengths[n] counts the real tokens of sentence n; slots from lengths[n] on are padding.
All inputs are finite; a program needn't handle non-finite values.
Results may differ from a plain program's by a relative error of at most 0.01.
Values may be sent and summed in bfloat16 or wider, within the bound.
A program may use at most 192 MiB of HBM per device.

v0:
```python
import functools
import math

import jax
import jax.numpy as jnp
from jax import lax
from jax.experimental import pallas as pl
from jax.experimental.pallas import tpu as pltpu
from jax.sharding import PartitionSpec as P

AX = ("dp", "fsdp")
MESH = pl.DeviceIdType.MESH
D = 768
H = 12
HD = 64
FF = 3072
LEN = 512
E2 = 512
E3 = 256
E4 = 128
E5 = 64


epsilon = 1e-05


PAR=7088640; LN=128
class Plan: pass
def plan(n):
    p=Plan(); p.n=n; p.sh=PAR//n
    st=[i*p.sh for i in range(n)]
    p.g0=[s//LN//16 for s in st]
    p.g1=[(s+p.sh-1)//LN//16 for s in st]
    p.slot=16*max(b-a+1 for a,b in zip(p.g0,p.g1))
    p.rows_in=-(-p.sh//LN)
    return p
MATS=[("wqkv",0,D,18),("wo",13836,D,6),("w1",18462,D,24),("w2",36918,FF,6)]
VECS=[(13824,12),(18444,18),(36894,24),(55350,30)]

def build_slot_kernel(p,me_of,x_ref,o_ref,q_ref):
    i=me_of(); start=i*p.sh; r_first=start//LN; s=start-r_first*LN; r0=r_first%16
    lead=32
    q_ref[...]=jnp.zeros_like(q_ref)
    q=pltpu.roll(x_ref[...].astype(jnp.float32),s,1)
    q_ref[lead:lead+p.rows_in]=q
    lane=lax.broadcasted_iota(jnp.int32,(p.slot,LN),1)
    a=q_ref[pl.ds(lead-r0,p.slot),:]
    b=q_ref[pl.ds(lead-1-r0,p.slot),:]
    o_ref[...]=jnp.where(lane>=s,a,b).astype(jnp.bfloat16)

def build_slot(p,shard,me_of):
    x=jnp.pad(shard,(0,p.rows_in*LN-p.sh)).reshape(p.rows_in,LN)
    return pl.pallas_call(functools.partial(build_slot_kernel,p,me_of),out_shape=jax.ShapeDtypeStruct((p.slot,LN),jnp.bfloat16),
        scratch_shapes=[pltpu.VMEM((32+p.slot+32,LN),jnp.float32)])(x)

def load_flat(p,slots,F,g_lo,g_hi):
    for i in range(p.n):
        a=max(g_lo,p.g0[i]); b=min(g_hi,p.g1[i]+1)
        if a>=b: continue
        shared_first = i>0 and p.g0[i]==p.g1[i-1] and a==p.g0[i]
        a2=a+1 if shared_first else a
        b2=b
        if i+1<p.n and p.g1[i]==p.g0[i+1] and b==p.g1[i]+1: b2=b-1
        if i+1<p.n and b2<b and b-1>=g_lo:
            g=b-1
            F[16*(g-g_lo):16*(g-g_lo)+16]=slots[i,16*(g-p.g0[i]):16*(g-p.g0[i])+16].astype(jnp.float32)+slots[i+1,0:16].astype(jnp.float32)
        cnt=b2-a2
        if cnt<=0: continue
        U=16
        nb,rem=cnt//U,cnt%U
        def body(t,_,i=i,a2=a2):
            src=pl.multiple_of(16*(a2-p.g0[i])+t*16*U,16); dst=pl.multiple_of(16*(a2-g_lo)+t*16*U,16)
            F[pl.ds(dst,16*U)]=slots[i,pl.ds(src,16*U)].astype(jnp.float32)
            return 0
        lax.fori_loop(0,nb,body,0)
        if rem:
            src=16*(a2-p.g0[i])+nb*16*U; dst=16*(a2-g_lo)+nb*16*U
            F[dst:dst+16*rem]=slots[i,src:src+16*rem].astype(jnp.float32)
def tile_matrix(F,W,off,rows,w,RB=64):
    def body(t,_):
        r=pl.multiple_of(t*RB,RB)
        for j in range(w):
            W[pl.ds(r,RB),j*LN:(j+1)*LN]=F[pl.ds(off+r*w+j,RB,stride=w),:].astype(jnp.bfloat16)
        return 0
    lax.fori_loop(0,rows//RB,body,0)
def relayout_kernel(p,slots,wqkv,wo,w1,w2,vec,F):
    outs=dict(wqkv=wqkv,wo=wo,w1=w1,w2=w2)
    for name,base,rows,w in MATS:
        g_lo=base//16; g_hi=-(-(base+rows*w)//16)
        load_flat(p,slots,F,g_lo,g_hi)
        tile_matrix(F,outs[name],base-16*g_lo,rows,w)
    at=0
    for base,cnt in VECS:
        g_lo=base//16; g_hi=-(-(base+cnt)//16)
        load_flat(p,slots,F,g_lo,g_hi)
        vec[at:at+cnt]=F[base-16*g_lo:base-16*g_lo+cnt]
        at+=cnt
def relayout(p,slots):
    shp=[jax.ShapeDtypeStruct((r,w*LN),jnp.bfloat16) for _,_,r,w in MATS]+[jax.ShapeDtypeStruct((84,LN),jnp.float32)]
    return pl.pallas_call(functools.partial(relayout_kernel,p),out_shape=shp,
        scratch_shapes=[pltpu.VMEM((18432+32,LN),jnp.float32)],
        compiler_params=pltpu.CompilerParams(vmem_limit_bytes=58<<20))(slots)

def coords():
    dp=lax.axis_index("dp"); fs=lax.axis_index("fsdp")
    return dp//2,fs%2,fs//2,dp%2
def dev(x,y,z,c): return (x*2+c, z*2+y)
def lin(x,y,z,c): return (x*2+c)*8+z*2+y
def barrier(partners):
    bar=pltpu.get_barrier_semaphore()
    for q in partners: pl.semaphore_signal(bar,inc=1,device_id=q,device_id_type=MESH)
    pl.semaphore_wait(bar,len(partners))
def gather_kernel(p,slot_ref,G,ssem,rsem,lsem):
    x,y,z,c=coords(); me=lin(x,y,z,c)
    half=p.slot//32*16
    H=((0,half),(half,p.slot-half))
    px,py,pc=dev(1-x,y,z,c),dev(x,1-y,z,c),dev(x,y,z,1-c)
    def zz(d):
        if d==1: return z+1-2*(z%2)
        if d==2: return lax.rem(z+2,4)
        return 3-z
    barrier([px,py,pc]+[dev(x,y,zz(d),c) for d in (1,2,3)])
    n_send=[0]; pend=[]
    def send(src,dst,to,sl,h,who):
        r0,rn=(H[h] if h<2 else (0,p.slot))
        k=n_send[0]; n_send[0]+=1
        cp=pltpu.make_async_remote_copy(src_ref=src(r0,rn),dst_ref=G.at[sl,pl.ds(r0,rn)],send_sem=ssem.at[k],recv_sem=rsem.at[sl,h],device_id=to,device_id_type=MESH)
        cp.start(); pend.append(cp)
    def wait(sl,h):
        r0,rn=(H[h] if h<2 else (0,p.slot))
        pltpu.make_async_copy(G.at[sl,pl.ds(r0,rn)],G.at[sl,pl.ds(r0,rn)],rsem.at[sl,h]).wait()
    def from_own(r0,rn): return slot_ref.at[pl.ds(r0,rn)]
    def from_g(sl): return lambda r0,rn: G.at[sl,pl.ds(r0,rn)]
    for to in (px,py,dev(x,y,zz(1),c),dev(x,y,zz(2),c),dev(x,y,zz(3),c),pc):
        send(from_own,None,to,me,2,None)
    loc=pltpu.make_async_copy(slot_ref,G.at[me],lsem); loc.start()
    def fwd_x(zq):
        sl=lin(1-x,y,zq,c); wait(sl,2); send(from_g(sl),None,py,sl,0,None); send(from_g(sl),None,pc,sl,2,None)
    def fwd_y(zq):
        sl=lin(x,1-y,zq,c); wait(sl,2); send(from_g(sl),None,px,sl,1,None); send(from_g(sl),None,pc,sl,2,None)
    def fwd_z(zq):
        sl=lin(x,y,zq,c); wait(sl,2)
        for to in (px,py,pc): send(from_g(sl),None,to,sl,2,None)
    def fwd_d(zq):
        sl=lin(1-x,1-y,zq,c)
        for h in (0,1):
            wait(sl,h); send(from_g(sl),None,pc,sl,h,None)
    fwd_x(z); fwd_y(z)
    for d in (1,3,2): fwd_z(zz(d))
    fwd_d(z)
    for d in (1,3,2): fwd_x(zz(d)); fwd_y(zz(d))
    for d in (1,3,2): fwd_d(zz(d))
    for zq in [z]+[zz(d) for d in (1,3,2)]:
        for (a,b) in ((x,y),(1-x,y),(x,1-y)): wait(lin(a,b,zq,1-c),2)
    for zq in [z]+[zz(d) for d in (1,3,2)]:
        for h in (0,1): wait(lin(1-x,1-y,zq,1-c),h)
    loc.wait()
    for cp in pend: cp.wait_send()
def gather(p,slot):
    return pl.pallas_call(functools.partial(gather_kernel,p),out_shape=jax.ShapeDtypeStruct((p.n,p.slot,LN),jnp.bfloat16),
        in_specs=[pl.BlockSpec(memory_space=pl.ANY)],out_specs=pl.BlockSpec(memory_space=pl.ANY),
        scratch_shapes=[pltpu.SemaphoreType.DMA((40,)),pltpu.SemaphoreType.DMA((p.n,3)),pltpu.SemaphoreType.DMA],
        compiler_params=pltpu.CompilerParams(collective_id=0,has_side_effects=True))(slot)

TOT=PAR//LN
def flat_rows(p): return max(16*p.g0[-1]+p.slot, EDGES[-1][0]+EDGES[-1][1])
def owner_row(rho):
    for k,(name,base,rows,w) in enumerate(MATS):
        if base<=rho<base+rows*w: return ("m",k,(rho-base)//w,(rho-base)%w)
    at=0
    for base,cnt in VECS:
        if base<=rho<base+cnt: return ("v",at+rho-base)
        at+=cnt
    return None
def untile_matrix(F,W,off,rows,w,RB=64):
    def body(t,_):
        r=pl.multiple_of(t*RB,RB)
        for j in range(w):
            F[pl.ds(off+r*w+j,RB,stride=w),:]=W[pl.ds(r,RB),j*LN:(j+1)*LN].astype(jnp.float32)
        return 0
    lax.fori_loop(0,rows//RB,body,0)
def store_flat(F,FG,f_row,g_row,rows,U=256):
    nb,rem=rows//U,rows%U
    def body(t,_):
        FG[pl.ds(pl.multiple_of(g_row+t*U,16),U)]=F[pl.ds(pl.multiple_of(f_row+t*U,16),U)].astype(jnp.bfloat16)
        return 0
    lax.fori_loop(0,nb,body,0)
    if rem: FG[g_row+nb*U:g_row+nb*U+rem]=F[f_row+nb*U:f_row+nb*U+rem].astype(jnp.bfloat16)
def flatten_kernel(p,wqkv,wo,w1,w2,vec,FG,F):
    ms=[wqkv,wo,w1,w2]
    end=flat_rows(p)
    def put(rho,lo):
        o=owner_row(rho)
        if o is None: F[rho-lo:rho-lo+1]=jnp.zeros((1,LN),jnp.float32)
        elif o[0]=="v": F[rho-lo:rho-lo+1]=vec[o[1]:o[1]+1]
        else: F[rho-lo:rho-lo+1]=ms[o[1]][o[2]:o[2]+1,o[3]*LN:(o[3]+1)*LN].astype(jnp.float32)
    cuts=[0,13824,18464,36928,end]
    for k,(name,base,rows,w) in enumerate(MATS):
        lo=cuts[k]//16*16; hi=cuts[k+1]
        f0=min(lo,base//16*16)
        untile_matrix(F,ms[k],base-f0,rows,w)
        for rho in list(range(lo,max(lo,base)))+list(range(base+rows*w,hi)): put(rho,f0)
        store_flat(F,FG,lo-f0,lo,hi-lo)
def flatten(p,dws,vec):
    return pl.pallas_call(functools.partial(flatten_kernel,p),out_shape=jax.ShapeDtypeStruct((flat_rows(p),LN),jnp.bfloat16),
        scratch_shapes=[pltpu.VMEM((18432+80,LN),jnp.float32)],
        compiler_params=pltpu.CompilerParams(vmem_limit_bytes=58<<20))(*dws,vec)

def scatter_kernel(p,FG,out,S,R,D0,D1,X,Y,Z,A,lsem,ssem,sib,dsem,xsem,ysem,zsem):
    x,y,z,c=coords(); me=lin(x,y,z,c)
    SL=p.slot
    half=SL//32*16
    px,py,pc=dev(1-x,y,z,c),dev(x,1-y,z,c),dev(x,y,z,1-c)
    def zz(d):
        if d==1: return z+1-2*(z%2)
        if d==2: return lax.rem(z+2,4)
        return 3-z
    pz={d:dev(x,y,zz(d),c) for d in (1,2,3)}
    pend=[]; ns=[0]
    def row0(i): return pl.multiple_of((i*p.sh)//LN//16*16,16)
    def send(src,dst,rsem,to):
        k=ns[0]; ns[0]+=1
        cp=pltpu.make_async_remote_copy(src_ref=src,dst_ref=dst,send_sem=ssem.at[k],recv_sem=rsem,device_id=to,device_id_type=MESH)
        cp.start(); pend.append(cp)
    def wait(ref,sem): pltpu.make_async_copy(ref,ref,sem).wait()
    zs=[zz(1),zz(2),zz(3),z]
    lines=[(1-x,1-y),(1-x,y),(x,1-y),(x,y)]
    for a,(xq,yq) in enumerate(lines):
        for b,zq in enumerate(zs):
            pltpu.make_async_copy(FG.at[pl.ds(row0(lin(xq,yq,zq,c)),SL)],S.at[4*a+b],lsem.at[4*a+b]).start()
    barrier([px,py,pc]+[pz[d] for d in (1,2,3)])
    for a,(xq,yq) in enumerate(lines):
        for b,zq in enumerate(zs):
            send(FG.at[pl.ds(row0(lin(xq,yq,zq,1-c)),SL)],R.at[4*a+b],sib.at[4*a+b],pc)
    U=176
    def add(dst,d0,rows,srcs):
        def body(t,_):
            r=pl.multiple_of(t*U,16)
            v=None
            for s,s0 in srcs:
                e=s[pl.ds(s0+r,U)].astype(jnp.float32); v=e if v is None else v+e
            dst[pl.ds(d0+r,U)]=v.astype(dst.dtype)
            return 0
        lax.fori_loop(0,rows//U,body,0)
    def have(k): wait(S.at[k],lsem.at[k]); wait(R.at[k],sib.at[k])
    for b in range(4):
        have(b)
        add(S.at[b],0,SL,[(S.at[b],0),(R.at[b],0)])
        send(S.at[b,pl.ds(0,half)],D0.at[b],dsem.at[0,b],py)
        send(S.at[b,pl.ds(half,SL-half)],D1.at[b],dsem.at[1,b],px)
    for b in range(4):
        k=4+b; have(k); wait(D0.at[b],dsem.at[0,b])
        add(S.at[k],0,half,[(S.at[k],0),(R.at[k],0),(D0.at[b],0)])
        add(S.at[k],half,SL-half,[(S.at[k],half),(R.at[k],half)])
        send(S.at[k],X.at[b],xsem.at[b],px)
        k=8+b; have(k); wait(D1.at[b],dsem.at[1,b])
        add(S.at[k],0,half,[(S.at[k],0),(R.at[k],0)])
        add(S.at[k],half,SL-half,[(S.at[k],half),(R.at[k],half),(D1.at[b],0)])
        send(S.at[k],Y.at[b],ysem.at[b],py)
    for b in range(4):
        k=12+b; have(k); wait(X.at[b],xsem.at[b]); wait(Y.at[b],ysem.at[b])
        if b<3:
            add(S.at[k],0,SL,[(S.at[k],0),(R.at[k],0),(X.at[b],0),(Y.at[b],0)])
            send(S.at[k],Z.at[b],zsem.at[b],pz[b+1])
    for b in range(3): wait(Z.at[b],zsem.at[b])
    add(A,0,SL,[(S.at[15],0),(R.at[15],0),(X.at[3],0),(Y.at[3],0),(Z.at[0],0),(Z.at[1],0),(Z.at[2],0)])
    start=me*p.sh; r_first=start//LN; s=start-r_first*LN; r0=r_first%16
    A[0:SL]=pltpu.roll(A[0:SL],lax.rem(LN-s,LN),1)
    lane=lax.broadcasted_iota(jnp.int32,(p.rows_in,LN),1)
    out[...]=jnp.where(lane<LN-s,A[pl.ds(r0,p.rows_in),:],A[pl.ds(r0+1,p.rows_in),:])
    for cp in pend: cp.wait_send()
def scatter(p,FG):
    SL=p.slot; half=SL//32*16; bf=jnp.bfloat16
    DM=pltpu.SemaphoreType.DMA
    o=pl.pallas_call(functools.partial(scatter_kernel,p),out_shape=jax.ShapeDtypeStruct((p.rows_in,LN),jnp.float32),
        in_specs=[pl.BlockSpec(memory_space=pl.ANY)],
        scratch_shapes=[pltpu.VMEM((16,SL,LN),bf),pltpu.VMEM((16,SL,LN),bf),pltpu.VMEM((4,half,LN),bf),pltpu.VMEM((4,SL-half,LN),bf),
            pltpu.VMEM((4,SL,LN),bf),pltpu.VMEM((4,SL,LN),bf),pltpu.VMEM((3,SL,LN),bf),pltpu.VMEM((SL+32,LN),jnp.float32),
            DM((16,)),DM((40,)),DM((16,)),DM((2,4)),DM((4,)),DM((4,)),DM((3,))],
        compiler_params=pltpu.CompilerParams(collective_id=1,has_side_effects=True,vmem_limit_bytes=58<<20))(FG)
    return o.reshape(-1)[:p.sh]

def me_of():
    return lax.axis_index(AX)


def finish_kernel(p, a_ref, out, A):
    SL = p.slot
    start = me_of() * p.sh
    r_first = start // LN
    s = start - r_first * LN
    r0 = r_first % 16
    A[0:SL] = pltpu.roll(a_ref[...], lax.rem(LN - s, LN), 1)
    lane = lax.broadcasted_iota(jnp.int32, (p.rows_in, LN), 1)
    out[...] = jnp.where(lane < LN - s, A[pl.ds(r0, p.rows_in), :], A[pl.ds(r0 + 1, p.rows_in), :])


def scatter_plain(p, flat):
    parts = jnp.concatenate([flat[16 * g : 16 * g + p.slot] for g in p.g0]).astype(jnp.float32)
    mine = lax.psum_scatter(parts, AX, scatter_dimension=0, tiled=True)
    o = pl.pallas_call(
        functools.partial(finish_kernel, p),
        out_shape=jax.ShapeDtypeStruct((p.rows_in, LN), jnp.float32),
        scratch_shapes=[pltpu.VMEM((p.slot + 32, LN), jnp.float32)],
    )(mine)
    return o.reshape(-1)[: p.sh]

EPS = 1e-05
F32 = jnp.float32
BF = jnp.bfloat16
SQ = math.sqrt(0.5)
PHI = 1.0 / math.sqrt(2.0 * math.pi)
VNAMES = (
    ("q_bias", D),
    ("v_bias", D),
    ("out_bias", D),
    ("first_gain", D),
    ("first_shift", D),
    ("up_bias", FF),
    ("down_bias", D),
    ("second_gain", D),
    ("second_shift", D),
    ("exit_gain", D),
    ("exit_shift", D),
)
VI = {name: k for k, (name, _) in enumerate(VNAMES)}
PREFIXES = (D, E2, E3, E4, E5)


def mm(a, b):
    return jnp.dot(a, b, preferred_element_type=F32)


def mm_nt(a, b):
    return lax.dot_general(a, b, (((1,), (1,)), ((), ())), preferred_element_type=F32)


def mm_tn(a, b):
    return lax.dot_general(a, b, (((0,), (0,)), ((), ())), preferred_element_type=F32)


def vrow(V, name):
    k = VI[name]
    return V[k : k + 1, : VNAMES[k][1]]


def mean_last(a):
    return jnp.mean(a, axis=-1, keepdims=True)


def sum_rows(a):
    return jnp.sum(a, axis=0, keepdims=True)


def forward_qkv(r):
    bias = jnp.concatenate([vrow(r.V, "q_bias"), jnp.zeros((1, D), F32), vrow(r.V, "v_bias")], axis=1)
    r.qb[...] = bias

    def body(j, _):
        o = pl.ds(pl.multiple_of(j * 256, 256), 256)
        r.qkv[:, o] = (mm(r.tok[...], r.wqkv[:, o]) + r.qb[:, o]).astype(BF)
        return 0

    lax.fori_loop(0, 3 * D // 256, body, 0)


def half_lanes(h):
    lane = lax.broadcasted_iota(jnp.int32, (LEN, LN), 1)
    return lane < HD if h == 0 else lane >= HD


def pair(r, part, hp):
    return r.qkv[:, pl.ds(pl.multiple_of(part * D + hp * LN, LN), LN)]


def forward_heads(r, hp):
    q, k, v = pair(r, 0, hp), pair(r, 1, hp), pair(r, 2, hp)
    valid = lax.broadcasted_iota(jnp.int32, (1, LEN), 1) < r.length
    out = None
    lse_all = r.lse[...]
    lane = lax.broadcasted_iota(jnp.int32, (LEN, LN), 1)
    for h in range(2):
        qh = jnp.where(half_lanes(h), q, jnp.zeros_like(q))
        s = jnp.where(valid, mm_nt(qh, k) * 0.125, -1e9)
        m = jnp.max(s, axis=1, keepdims=True)
        e = jnp.exp(s - m)
        l = jnp.sum(e, axis=1, keepdims=True)
        low = (e * (1.0 / l)).astype(BF)
        o = mm(low, v)
        out = o if out is None else jnp.where(half_lanes(0), out, o)
        lse_all = jnp.where(lane == 2 * hp + h, m + jnp.log(l), lse_all)
    r.lse[...] = lse_all
    r.mixed[:, pl.ds(pl.multiple_of(hp * LN, LN), LN)] = out.astype(BF)


def rows_of(b, n):
    return pl.ds(pl.multiple_of(b * n, n), n)


def forward_first(r):
    def body(b, _):
        o = rows_of(b, 256)
        v = r.tok[o, :].astype(F32) + mm(r.mixed[o, :], r.wo[...]) + vrow(r.V, "out_bias")
        cen = v - mean_last(v)
        rstd = lax.rsqrt(mean_last(cen * cen) + EPS)
        xh = cen * rstd
        r.xh1[o, :] = xh
        r.rstd1[o, :] = rstd
        r.first_low[o, :] = (xh * vrow(r.V, "first_gain") + vrow(r.V, "first_shift")).astype(BF)
        return 0

    lax.fori_loop(0, LEN // 256, body, 0)


def forward_up(r, j):
    o = pl.ds(pl.multiple_of(j * 256, 256), 256)
    v = mm(r.first_low[...], r.w1[:, o]) + r.V[VI["up_bias"] : VI["up_bias"] + 1, o]
    cdf = 0.5 * (1.0 + lax.erf(v * SQ))
    r.act[:, o] = (v * cdf).astype(BF)
    r.gd[:, o] = (cdf + v * (PHI * jnp.exp(-0.5 * v * v))).astype(BF)


def forward_second(r):
    def body(b, tot):
        o = rows_of(b, 256)
        first = r.xh1[o, :] * vrow(r.V, "first_gain") + vrow(r.V, "first_shift")
        v = first + mm(r.act[o, :], r.w2[...]) + vrow(r.V, "down_bias")
        cen = v - mean_last(v)
        rstd = lax.rsqrt(mean_last(cen * cen) + EPS)
        xh = cen * rstd
        r.xh2[o, :] = xh
        r.rstd2[o, :] = rstd
        t = lax.broadcasted_iota(jnp.int32, (256, 1), 0) + b * 256
        hid = (xh * vrow(r.V, "second_gain") + vrow(r.V, "second_shift")) * (t < r.length).astype(F32)
        r.hidden[o, :] = hid.astype(BF)
        return tot + sum_rows(hid)

    return lax.fori_loop(0, LEN // 256, body, jnp.zeros((1, D), F32))


def head(r, tot):
    inv_len = 1.0 / jnp.full((1, 1), r.length, jnp.int32).astype(F32)
    pooled = tot * inv_len
    cen = pooled - mean_last(pooled)
    rstd = lax.rsqrt(mean_last(cen * cen) + EPS)
    xh = cen * rstd
    gain = vrow(r.V, "exit_gain")
    emb = xh * gain + vrow(r.V, "exit_shift")
    d_emb = jnp.zeros((1, D), F32)
    at = 0
    for m in PREFIXES:
        e = emb[:, :m]
        inv = lax.rsqrt(jnp.sum(e * e, axis=1, keepdims=True) * (1.0 / m) + EPS)
        out = e * inv
        r.nested[:, at : at + m] = out
        c = r.ncot[:, at : at + m]
        g = inv * (c - out * (jnp.sum(c * out, axis=1, keepdims=True) * (1.0 / m)))
        d_emb = d_emb + (g if m == D else jnp.concatenate([g, jnp.zeros((1, D - m), F32)], axis=1))
        at += m
    put_grad(r, "exit_gain", d_emb * xh)
    put_grad(r, "exit_shift", d_emb)
    dx = d_emb * gain
    return rstd * (dx - mean_last(dx) - xh * mean_last(dx * xh)) * inv_len


def put_grad(r, name, value):
    k = VI[name]
    r.VG[k : k + 1, : VNAMES[k][1]] = value


def norm_back(dy, gain, xh, rstd):
    dx = dy * gain
    return rstd * (dx - mean_last(dx) - xh * mean_last(dx * xh))


def backward_second(r, d_pool):
    def body(b, c):
        o = rows_of(b, 128)
        t = lax.broadcasted_iota(jnp.int32, (128, 1), 0) + b * 128
        dy = (r.hcot[o, :].astype(F32) + d_pool) * (t < r.length).astype(F32)
        xh = r.xh2[o, :]
        res = norm_back(dy, vrow(r.V, "second_gain"), xh, r.rstd2[o, :])
        r.res[o, :] = res
        low = res.astype(BF)
        r.d_outer[o, :] = low
        return (c[0] + sum_rows(dy * xh), c[1] + sum_rows(dy), c[2] + sum_rows(low.astype(F32)))

    z = jnp.zeros((1, D), F32)
    a, b, c = lax.fori_loop(0, LEN // 128, body, (z, z, z))
    put_grad(r, "second_gain", a)
    put_grad(r, "second_shift", b)
    put_grad(r, "down_bias", c)


def backward_act(r, j):
    o = pl.ds(pl.multiple_of(j * 256, 256), 256)
    d = (mm_nt(r.d_outer[...], r.w2[o, :]) * r.gd[:, o].astype(F32)).astype(BF)
    r.gd[:, o] = d
    r.VG[VI["up_bias"] : VI["up_bias"] + 1, o] = sum_rows(d.astype(F32))


def backward_first(r):
    def body(b, c):
        o = rows_of(b, 256)
        dy = mm_nt(r.gd[o, :], r.w1[...]) + r.res[o, :]
        xh = r.xh1[o, :]
        res = norm_back(dy, vrow(r.V, "first_gain"), xh, r.rstd1[o, :])
        r.res[o, :] = res
        low = res.astype(BF)
        r.d_branch[o, :] = low
        return (c[0] + sum_rows(dy * xh), c[1] + sum_rows(dy), c[2] + sum_rows(low.astype(F32)))

    z = jnp.zeros((1, D), F32)
    a, b, c = lax.fori_loop(0, LEN // 256, body, (z, z, z))
    put_grad(r, "first_gain", a)
    put_grad(r, "first_shift", b)
    put_grad(r, "out_bias", c)


def backward_mixed(r):
    r.d_mixed[...] = mm_nt(r.d_branch[...], r.wo[...]).astype(BF)


def backward_heads(r, hp):
    q, k, v = pair(r, 0, hp), pair(r, 1, hp), pair(r, 2, hp)
    cols = pl.ds(pl.multiple_of(hp * LN, LN), LN)
    dm = r.d_mixed[:, cols]
    valid = lax.broadcasted_iota(jnp.int32, (1, LEN), 1) < r.length
    lane = lax.broadcasted_iota(jnp.int32, (LEN, LN), 1)
    zero = jnp.zeros_like(q)
    dq = dk = dv = None
    for h in range(2):
        here = half_lanes(h)
        qh, kh, dmh = jnp.where(here, q, zero), jnp.where(here, k, zero), jnp.where(here, dm, zero)
        lse = jnp.sum(jnp.where(lane == 2 * hp + h, r.lse[...], 0.0), axis=1, keepdims=True)
        s = jnp.where(valid, mm_nt(qh, k) * 0.125, -1e9)
        p = jnp.exp(s - lse)
        dp = mm_nt(dmh, v)
        ds = (p * (dp - jnp.sum(dp * p, axis=1, keepdims=True))).astype(BF)
        a, b, c = mm(ds, kh), mm_tn(ds, qh), mm_tn(p.astype(BF), dmh)
        dq, dk, dv = (a, b, c) if dq is None else (dq + a, dk + b, dv + c)
    dq, dk, dv = (dq * 0.125).astype(BF), (dk * 0.125).astype(BF), dv.astype(BF)
    for part, g in ((0, dq), (1, dk), (2, dv)):
        r.dqkv[:, pl.ds(pl.multiple_of(part * D + hp * LN, LN), LN)] = g
    k = VI["q_bias"]
    r.VG[k : k + 1, cols] = sum_rows(dq.astype(F32))
    k = VI["v_bias"]
    r.VG[k : k + 1, cols] = sum_rows(dv.astype(F32))


def backward_tokens(r, b):
    o = rows_of(b, 128)
    v = r.res[o, :]
    for part in range(3):
        v = v + mm_nt(r.dqkv[o, part * D : (part + 1) * D], r.wqkv[:, part * D : (part + 1) * D])
    r.res[o, :] = v


EDGES = ((13824, 16), (18432, 32), (36880, 48), (55344, 64))


def edge_at(row):
    at = 0
    for base, rows in EDGES:
        if base <= row < base + rows:
            return at + row - base
        at += rows
    return None


def weight_grad(r, lhs, rhs, base, rows, w, RB=256, CB=6):
    lead = base % 16
    step_rows = RB * w
    F = r.F
    if lead:
        F[0:16] = jnp.zeros((16, LN), F32)

    def body(s, _):
        o = pl.ds(pl.multiple_of(s * RB, RB), RB)
        for ch in range(w // CB):
            g = mm_tn(lhs[:, o], rhs[:, ch * CB * LN : (ch + 1) * CB * LN])
            for j in range(CB):
                F[pl.ds(lead + ch * CB + j, RB, stride=w), :] = g[:, j * LN : (j + 1) * LN]
        if lead:
            @pl.when(s == 0)
            def _():
                e = edge_at(base)
                r.E[e : e + 16 - lead] = F[lead:16]

        U = 256
        to = base - lead + s * step_rows

        def emit(t, _):
            r.FG[pl.ds(pl.multiple_of(to + t * U, 16), U)] = F[pl.ds(pl.multiple_of(t * U, 16), U)].astype(BF)
            return 0

        lax.fori_loop(0, step_rows // U, emit, 0)
        if lead:
            F[0:16] = F[step_rows : step_rows + 16]
        return 0

    lax.fori_loop(0, rows // RB, body, 0)
    if lead:
        e = edge_at(base + rows * w - lead)
        r.E[e : e + lead] = F[0:lead]


def edge_grads(r, which):
    base, rows = EDGES[which]
    at = 0
    for vbase, cnt in VECS:
        for k in range(cnt):
            row = vbase + k
            if base <= row < base + rows:
                name, j = vec_at(at + k)
                e = edge_at(row)
                r.E[e : e + 1] = r.VG[name : name + 1, j * LN : (j + 1) * LN]
        at += cnt
    if which == len(EDGES) - 1:
        e = edge_at(TOT)
        r.E[e : e + base + rows - TOT] = jnp.zeros((base + rows - TOT, LN), F32)
    e = edge_at(base)
    r.FG[base : base + rows] = r.E[e : e + rows].astype(BF)


def vec_at(row):
    for k, (_, n) in enumerate(VNAMES):
        if row < n // LN:
            return k, row
        row -= n // LN


class Refs:
    def __init__(self, **refs):
        self.__dict__.update(refs)


def relayout_vectors(p, r):
    at = 0
    for base, cnt in VECS:
        g_lo = base // 16
        g_hi = -(-(base + cnt) // 16)
        load_flat(p, r.slots, r.F, g_lo, g_hi)
        for k in range(cnt):
            name, j = vec_at(at + k)
            f = base - 16 * g_lo + k
            r.V[name : name + 1, j * LN : (j + 1) * LN] = r.F[f : f + 1]
        at += cnt


def relayout_matrix(p, r, name, W, RB):
    base, rows, w = {n: (b, k, c) for n, b, k, c in MATS}[name]
    for s in range(rows // RB):
        lo = base + s * RB * w
        g_lo = lo // 16
        load_flat(p, r.slots, r.F, g_lo, -(-(lo + RB * w) // 16))
        tile_rows(r.F, W, lo - 16 * g_lo, s * RB, RB, w)


def tile_rows(F, W, off, row, rows, w, RB=64):
    def body(t, _):
        q = pl.multiple_of(t * RB, RB)
        for j in range(w):
            W[pl.ds(row + q, RB), j * LN : (j + 1) * LN] = F[pl.ds(off + q * w + j, RB, stride=w), :].astype(BF)
        return 0

    lax.fori_loop(0, rows // RB, body, 0)


def forward_kernel(p, slots, length, tok, hcot, ncot, hidden, nested, wqkv, wo, w1, w2, V, VG, qkv, lse, mixed, xh1, rstd1, first_low, act, gd, res, d_outer, F, qb, xh2, rstd2):
    r = Refs(slots=slots, length=length[0], tok=tok, hcot=hcot, ncot=ncot, hidden=hidden, nested=nested, wqkv=wqkv, wo=wo, w1=w1, w2=w2, V=V, VG=VG, qkv=qkv, lse=lse, mixed=mixed, xh1=xh1, rstd1=rstd1, first_low=first_low, act=act, gd=gd, res=res, d_outer=d_outer, F=F, qb=qb, xh2=xh2, rstd2=rstd2)
    relayout_vectors(p, r)
    relayout_matrix(p, r, "wqkv", wqkv, 256)
    forward_qkv(r)
    lse[...] = jnp.zeros_like(lse)
    lax.fori_loop(0, H // 2, lambda hp, c: (forward_heads(r, hp), c)[1], 0)
    relayout_matrix(p, r, "wo", wo, 768)
    forward_first(r)
    relayout_matrix(p, r, "w1", w1, 256)
    lax.fori_loop(0, FF // 256, lambda j, c: (forward_up(r, j), c)[1], 0)
    relayout_matrix(p, r, "w2", w2, 768)
    tot = forward_second(r)
    d_pool = head(r, tot)
    backward_second(r, d_pool)


def forward_local(p, slots, length, tok, hcot, ncot):
    S = jax.ShapeDtypeStruct
    outs = [S((LEN, D), BF), S((1, 1728), F32), S((D, 3 * D), BF), S((D, D), BF), S((D, FF), BF), S((FF, D), BF), S((16, FF), F32), S((16, FF), F32), S((LEN, 3 * D), BF), S((LEN, LN), F32), S((LEN, D), BF), S((LEN, D), F32), S((LEN, 1), F32), S((LEN, D), BF), S((LEN, FF), BF), S((LEN, FF), BF), S((LEN, D), F32), S((LEN, D), BF)]
    vm = pl.BlockSpec(memory_space=pltpu.VMEM)
    sm = pl.BlockSpec(memory_space=pltpu.SMEM)
    return pl.pallas_call(
        functools.partial(forward_kernel, p),
        out_shape=outs,
        in_specs=[vm, sm, vm, vm, vm],
        scratch_shapes=[pltpu.VMEM((6144 + 32, LN), F32), pltpu.VMEM((1, 3 * D), F32), pltpu.VMEM((LEN, D), F32), pltpu.VMEM((LEN, 1), F32)],
        compiler_params=pltpu.CompilerParams(vmem_limit_bytes=60 << 20),
    )(slots, length, tok, hcot, ncot)


def backward_kernel(p, length, tok, V, VG0, qkv, lse, mixed, xh1, rstd1, first_low, act, gd, res, d_outer, wqkv, wo, w1, w2, igrad, FG, VG, d_branch, d_mixed, dqkv, F, E):
    r = Refs(length=length[0], tok=tok, V=V, VG=VG, qkv=qkv, lse=lse, mixed=mixed, xh1=xh1, rstd1=rstd1, first_low=first_low, act=act, gd=gd, res=igrad, d_outer=d_outer, wqkv=wqkv, wo=wo, w1=w1, w2=w2, FG=FG, d_branch=d_branch, d_mixed=d_mixed, dqkv=dqkv, F=F, E=E)
    VG[...] = VG0[...]
    igrad[...] = res[...]
    mats = {n: (b, k, c) for n, b, k, c in MATS}
    weight_grad(r, act, d_outer, *mats["w2"])
    edge_grads(r, 3)
    lax.fori_loop(0, FF // 256, lambda j, c: (backward_act(r, j), c)[1], 0)
    weight_grad(r, first_low, gd, *mats["w1"])
    edge_grads(r, 2)
    backward_first(r)
    weight_grad(r, mixed, d_branch, *mats["wo"])
    edge_grads(r, 1)
    backward_mixed(r)
    lax.fori_loop(0, H // 2, lambda hp, c: (backward_heads(r, hp), c)[1], 0)
    weight_grad(r, tok, dqkv, *mats["wqkv"])
    edge_grads(r, 0)
    lax.fori_loop(0, LEN // 128, lambda b, c: (backward_tokens(r, b), c)[1], 0)


def backward_local(p, length, tok, V, VG, qkv, lse, mixed, xh1, rstd1, first_low, act, gd, res, d_outer, wqkv, wo, w1, w2):
    S = jax.ShapeDtypeStruct
    vm = pl.BlockSpec(memory_space=pltpu.VMEM)
    sm = pl.BlockSpec(memory_space=pltpu.SMEM)
    return pl.pallas_call(
        functools.partial(backward_kernel, p),
        out_shape=[S((LEN, D), F32), S((flat_rows(p), LN), BF)],
        in_specs=[sm] + [vm] * 17,
        scratch_shapes=[pltpu.VMEM((16, FF), F32), pltpu.VMEM((LEN, D), BF), pltpu.VMEM((LEN, D), BF), pltpu.VMEM((LEN, 3 * D), BF), pltpu.VMEM((6144 + 32, LN), F32), pltpu.VMEM((160, LN), F32)],
        compiler_params=pltpu.CompilerParams(vmem_limit_bytes=60 << 20),
    )(length, tok, V, VG, qkv, lse, mixed, xh1, rstd1, first_low, act, gd, res, d_outer, wqkv, wo, w1, w2)


def on_device(p, fast, tokens, lengths, weight_shards, hidden_cotangent, nested_cotangent):
    slot = build_slot(p, weight_shards, me_of)
    slots = gather(p, slot) if fast else lax.all_gather(slot, AX, axis=0)
    tok = tokens.reshape(LEN, D)
    (hidden, nested, wqkv, wo, w1, w2, V, VG, qkv, lse, mixed, xh1, rstd1, first_low, act, gd, res, d_outer) = forward_local(p, slots, lengths, tok, hidden_cotangent.reshape(LEN, D), nested_cotangent)
    igrad, flat = backward_local(p, lengths, tok, V, VG, qkv, lse, mixed, xh1, rstd1, first_low, act, gd, res, d_outer, wqkv, wo, w1, w2)
    shards = scatter(p, flat) if fast else scatter_plain(p, flat)
    return (hidden.reshape(1, LEN, D), nested, igrad.reshape(1, LEN, D), shards)


def solution(mesh):
    in_specs = (
        P(("dp", "fsdp"), None, None),
        P(("dp", "fsdp")),
        P(("dp", "fsdp")),
        P(("dp", "fsdp"), None, None),
        P(("dp", "fsdp"), None),
    )
    out_specs = (
        P(("dp", "fsdp"), None, None),
        P(("dp", "fsdp"), None),
        P(("dp", "fsdp"), None, None),
        P(("dp", "fsdp")),
    )
    p = plan(mesh.shape["dp"] * mesh.shape["fsdp"])
    fast = (mesh.shape["dp"], mesh.shape["fsdp"]) == (4, 8)
    return jax.shard_map(
        functools.partial(on_device, p, fast), mesh=mesh, in_specs=in_specs, out_specs=out_specs, check_vma=False
    )
```

profile of v0, /device:TPU:11, one launch (start us, length us, event | category | flops | bytes accessed | tf_op | source)
XLA Modules:
  0.0 280.4 jit_solution(6323061740102462829)
XLA Ops:
  1.3 1.8 pad_bitcast_fusion.x_ref
  3.1 2.1 shard_map.84.slot_ref
  5.2 81.8 %shard_map.85.slots = bf16[32,1760,128]{2,1,0:T(8,128)(2,1)} custom-call(bf16[1760,128]{1,0:T(8,128)(2,1)} %shard_map.84.slot_ref), custom_call_target="tpu_custom_call" | custom-call | tf_op jit(solution)/shard_map/pallas_call | solution.py:160
  86.9 46.1 %shard_map.86 = (bf16[512,768]{1,0:T(8,128)(2,1)}, f32[1,1728]{1,0:T(1,128)}, bf16[768,2304]{1,0:T(8,128)(2,1)}, bf16[768,768]{1,0:T(8,128)(2,1)}, bf16[768,3072...) custom-call(bf16[32,1760,128]{2,1,0:T(8,128)(2,1)} %shard_map.85.slo, ...), custom_call_target="tpu_custom_call" | custom-call | tf_op jit(solution)/shard_map/pallas_call | solution.py:692
  133.0 58.2 %shard_map.87 = (f32[512,768]{1,0:T(8,128)}, bf16[55408,128]{1,0:T(8,128)(2,1)}) custom-call(s32[1]{0:T(128)S(6)} %copy.10.length, bf16[512,768]{1,0:T(8,128)(2,1)} %bitcast.10, f32[16,3072]{1,0:T(8,128)} %get-tuple-element.26.V, f32[16,3072]{1,0:T(8,128)} %get-tuple-element.27.VG0, bf16[512,2304]{1,0:T(8,128)(2,1)} %get-tuple-element.28.qkv, ...), custom_call_target="tpu_custom_call" | custom-call | tf_op jit(solution)/shard_map/pallas_call | solution.py:725
  191.2 87.1 %shard_map.88 = f32[1731,128]{1,0:T(8,128)} custom-call(bf16[55408,128]{1,0:T(8,128)(2,1)} %get-tuple-element.43.FG), custom_call_target="tpu_custom_call" | custom-call | tf_op jit(solution)/shard_map/pallas_call | solution.py:275
  278.3 2.1 copy.11
where the time goes:
time: 281 us; the launch traced here: 280 us
  Pallas kernels  275 us (98%)
  local copies, waits for them, and re-layouts  3.95 us (1%)
    pallas_call x1, Pallas kernels, scatter(): pl.pallas_call(functools.partial(scatter_kernel, p), out_shape=jax.ShapeD...  87.1 us
    pallas_call x1, Pallas kernels, gather(): pl.pallas_call(functools.partial(gather_kernel, p), out_shape=jax.ShapeDt...  81.8 us
    pallas_call x1, Pallas kernels, backward_local(): pl.pallas_call(functools.partial(backward_kernel, p), out_shape=[S((LEN,...  58.2 us
    pallas_call x1, Pallas kernels, forward_local(): pl.pallas_call(functools.partial(forward_kernel, p), out_shape=outs, in_s...  46.1 us

commit v1 on v0

--- a/solution.py
+++ b/solution.py
@@ -53,14 +53,15 @@
     return pl.pallas_call(functools.partial(build_slot_kernel,p,me_of),out_shape=jax.ShapeDtypeStruct((p.slot,LN),jnp.bfloat16),
         scratch_shapes=[pltpu.VMEM((32+p.slot+32,LN),jnp.float32)])(x)
 
-def load_flat(p,slots,F,g_lo,g_hi):
+def load_flat(p,slots,F,g_lo,g_hi,need=None):
     for i in range(p.n):
         a=max(g_lo,p.g0[i]); b=min(g_hi,p.g1[i]+1)
         if a>=b: continue
         shared_first = i>0 and p.g0[i]==p.g1[i-1] and a==p.g0[i]
         a2=a+1 if shared_first else a
         b2=b
-        if i+1<p.n and p.g1[i]==p.g0[i+1] and b==p.g1[i]+1: b2=b-1
+        apart=need is not None and need<=(i+1)*p.sh//LN
+        if i+1<p.n and p.g1[i]==p.g0[i+1] and b==p.g1[i]+1 and not apart: b2=b-1
         if i+1<p.n and b2<b and b-1>=g_lo:
             g=b-1
             F[16*(g-g_lo):16*(g-g_lo)+16]=slots[i,16*(g-p.g0[i]):16*(g-p.g0[i])+16].astype(jnp.float32)+slots[i+1,0:16].astype(jnp.float32)
@@ -76,30 +77,6 @@
         if rem:
             src=16*(a2-p.g0[i])+nb*16*U; dst=16*(a2-g_lo)+nb*16*U
             F[dst:dst+16*rem]=slots[i,src:src+16*rem].astype(jnp.float32)
-def tile_matrix(F,W,off,rows,w,RB=64):
-    def body(t,_):
-        r=pl.multiple_of(t*RB,RB)
-        for j in range(w):
-            W[pl.ds(r,RB),j*LN:(j+1)*LN]=F[pl.ds(off+r*w+j,RB,stride=w),:].astype(jnp.bfloat16)
-        return 0
-    lax.fori_loop(0,rows//RB,body,0)
-def relayout_kernel(p,slots,wqkv,wo,w1,w2,vec,F):
-    outs=dict(wqkv=wqkv,wo=wo,w1=w1,w2=w2)
-    for name,base,rows,w in MATS:
-        g_lo=base//16; g_hi=-(-(base+rows*w)//16)
-        load_flat(p,slots,F,g_lo,g_hi)
-        tile_matrix(F,outs[name],base-16*g_lo,rows,w)
-    at=0
-    for base,cnt in VECS:
-        g_lo=base//16; g_hi=-(-(base+cnt)//16)
-        load_flat(p,slots,F,g_lo,g_hi)
-        vec[at:at+cnt]=F[base-16*g_lo:base-16*g_lo+cnt]
-        at+=cnt
-def relayout(p,slots):
-    shp=[jax.ShapeDtypeStruct((r,w*LN),jnp.bfloat16) for _,_,r,w in MATS]+[jax.ShapeDtypeStruct((84,LN),jnp.float32)]
-    return pl.pallas_call(functools.partial(relayout_kernel,p),out_shape=shp,
-        scratch_shapes=[pltpu.VMEM((18432+32,LN),jnp.float32)],
-        compiler_params=pltpu.CompilerParams(vmem_limit_bytes=58<<20))(slots)
 
 def coords():
     dp=lax.axis_index("dp"); fs=lax.axis_index("fsdp")
@@ -110,57 +87,6 @@
     bar=pltpu.get_barrier_semaphore()
     for q in partners: pl.semaphore_signal(bar,inc=1,device_id=q,device_id_type=MESH)
     pl.semaphore_wait(bar,len(partners))
-def gather_kernel(p,slot_ref,G,ssem,rsem,lsem):
-    x,y,z,c=coords(); me=lin(x,y,z,c)
-    half=p.slot//32*16
-    H=((0,half),(half,p.slot-half))
-    px,py,pc=dev(1-x,y,z,c),dev(x,1-y,z,c),dev(x,y,z,1-c)
-    def zz(d):
-        if d==1: return z+1-2*(z%2)
-        if d==2: return lax.rem(z+2,4)
-        return 3-z
-    barrier([px,py,pc]+[dev(x,y,zz(d),c) for d in (1,2,3)])
-    n_send=[0]; pend=[]
-    def send(src,dst,to,sl,h,who):
-        r0,rn=(H[h] if h<2 else (0,p.slot))
-        k=n_send[0]; n_send[0]+=1
-        cp=pltpu.make_async_remote_copy(src_ref=src(r0,rn),dst_ref=G.at[sl,pl.ds(r0,rn)],send_sem=ssem.at[k],recv_sem=rsem.at[sl,h],device_id=to,device_id_type=MESH)
-        cp.start(); pend.append(cp)
-    def wait(sl,h):
-        r0,rn=(H[h] if h<2 else (0,p.slot))
-        pltpu.make_async_copy(G.at[sl,pl.ds(r0,rn)],G.at[sl,pl.ds(r0,rn)],rsem.at[sl,h]).wait()
-    def from_own(r0,rn): return slot_ref.at[pl.ds(r0,rn)]
-    def from_g(sl): return lambda r0,rn: G.at[sl,pl.ds(r0,rn)]
-    for to in (px,py,dev(x,y,zz(1),c),dev(x,y,zz(2),c),dev(x,y,zz(3),c),pc):
-        send(from_own,None,to,me,2,None)
-    loc=pltpu.make_async_copy(slot_ref,G.at[me],lsem); loc.start()
-    def fwd_x(zq):
-        sl=lin(1-x,y,zq,c); wait(sl,2); send(from_g(sl),None,py,sl,0,None); send(from_g(sl),None,pc,sl,2,None)
-    def fwd_y(zq):
-        sl=lin(x,1-y,zq,c); wait(sl,2); send(from_g(sl),None,px,sl,1,None); send(from_g(sl),None,pc,sl,2,None)
-    def fwd_z(zq):
-        sl=lin(x,y,zq,c); wait(sl,2)
-        for to in (px,py,pc): send(from_g(sl),None,to,sl,2,None)
-    def fwd_d(zq):
-        sl=lin(1-x,1-y,zq,c)
-        for h in (0,1):
-            wait(sl,h); send(from_g(sl),None,pc,sl,h,None)
-    fwd_x(z); fwd_y(z)
-    for d in (1,3,2): fwd_z(zz(d))
-    fwd_d(z)
-    for d in (1,3,2): fwd_x(zz(d)); fwd_y(zz(d))
-    for d in (1,3,2): fwd_d(zz(d))
-    for zq in [z]+[zz(d) for d in (1,3,2)]:
-        for (a,b) in ((x,y),(1-x,y),(x,1-y)): wait(lin(a,b,zq,1-c),2)
-    for zq in [z]+[zz(d) for d in (1,3,2)]:
-        for h in (0,1): wait(lin(1-x,1-y,zq,1-c),h)
-    loc.wait()
-    for cp in pend: cp.wait_send()
-def gather(p,slot):
-    return pl.pallas_call(functools.partial(gather_kernel,p),out_shape=jax.ShapeDtypeStruct((p.n,p.slot,LN),jnp.bfloat16),
-        in_specs=[pl.BlockSpec(memory_space=pl.ANY)],out_specs=pl.BlockSpec(memory_space=pl.ANY),
-        scratch_shapes=[pltpu.SemaphoreType.DMA((40,)),pltpu.SemaphoreType.DMA((p.n,3)),pltpu.SemaphoreType.DMA],
-        compiler_params=pltpu.CompilerParams(collective_id=0,has_side_effects=True))(slot)
 
 TOT=PAR//LN
 def flat_rows(p): return max(16*p.g0[-1]+p.slot, EDGES[-1][0]+EDGES[-1][1])
@@ -172,113 +98,6 @@
         if base<=rho<base+cnt: return ("v",at+rho-base)
         at+=cnt
     return None
-def untile_matrix(F,W,off,rows,w,RB=64):
-    def body(t,_):
-        r=pl.multiple_of(t*RB,RB)
-        for j in range(w):
-            F[pl.ds(off+r*w+j,RB,stride=w),:]=W[pl.ds(r,RB),j*LN:(j+1)*LN].astype(jnp.float32)
-        return 0
-    lax.fori_loop(0,rows//RB,body,0)
-def store_flat(F,FG,f_row,g_row,rows,U=256):
-    nb,rem=rows//U,rows%U
-    def body(t,_):
-        FG[pl.ds(pl.multiple_of(g_row+t*U,16),U)]=F[pl.ds(pl.multiple_of(f_row+t*U,16),U)].astype(jnp.bfloat16)
-        return 0
-    lax.fori_loop(0,nb,body,0)
-    if rem: FG[g_row+nb*U:g_row+nb*U+rem]=F[f_row+nb*U:f_row+nb*U+rem].astype(jnp.bfloat16)
-def flatten_kernel(p,wqkv,wo,w1,w2,vec,FG,F):
-    ms=[wqkv,wo,w1,w2]
-    end=flat_rows(p)
-    def put(rho,lo):
-        o=owner_row(rho)
-        if o is None: F[rho-lo:rho-lo+1]=jnp.zeros((1,LN),jnp.float32)
-        elif o[0]=="v": F[rho-lo:rho-lo+1]=vec[o[1]:o[1]+1]
-        else: F[rho-lo:rho-lo+1]=ms[o[1]][o[2]:o[2]+1,o[3]*LN:(o[3]+1)*LN].astype(jnp.float32)
-    cuts=[0,13824,18464,36928,end]
-    for k,(name,base,rows,w) in enumerate(MATS):
-        lo=cuts[k]//16*16; hi=cuts[k+1]
-        f0=min(lo,base//16*16)
-        untile_matrix(F,ms[k],base-f0,rows,w)
-        for rho in list(range(lo,max(lo,base)))+list(range(base+rows*w,hi)): put(rho,f0)
-        store_flat(F,FG,lo-f0,lo,hi-lo)
-def flatten(p,dws,vec):
-    return pl.pallas_call(functools.partial(flatten_kernel,p),out_shape=jax.ShapeDtypeStruct((flat_rows(p),LN),jnp.bfloat16),
-        scratch_shapes=[pltpu.VMEM((18432+80,LN),jnp.float32)],
-        compiler_params=pltpu.CompilerParams(vmem_limit_bytes=58<<20))(*dws,vec)
-
-def scatter_kernel(p,FG,out,S,R,D0,D1,X,Y,Z,A,lsem,ssem,sib,dsem,xsem,ysem,zsem):
-    x,y,z,c=coords(); me=lin(x,y,z,c)
-    SL=p.slot
-    half=SL//32*16
-    px,py,pc=dev(1-x,y,z,c),dev(x,1-y,z,c),dev(x,y,z,1-c)
-    def zz(d):
-        if d==1: return z+1-2*(z%2)
-        if d==2: return lax.rem(z+2,4)
-        return 3-z
-    pz={d:dev(x,y,zz(d),c) for d in (1,2,3)}
-    pend=[]; ns=[0]
-    def row0(i): return pl.multiple_of((i*p.sh)//LN//16*16,16)
-    def send(src,dst,rsem,to):
-        k=ns[0]; ns[0]+=1
-        cp=pltpu.make_async_remote_copy(src_ref=src,dst_ref=dst,send_sem=ssem.at[k],recv_sem=rsem,device_id=to,device_id_type=MESH)
-        cp.start(); pend.append(cp)
-    def wait(ref,sem): pltpu.make_async_copy(ref,ref,sem).wait()
-    zs=[zz(1),zz(2),zz(3),z]
-    lines=[(1-x,1-y),(1-x,y),(x,1-y),(x,y)]
-    for a,(xq,yq) in enumerate(lines):
-        for b,zq in enumerate(zs):
-            pltpu.make_async_copy(FG.at[pl.ds(row0(lin(xq,yq,zq,c)),SL)],S.at[4*a+b],lsem.at[4*a+b]).start()
-    barrier([px,py,pc]+[pz[d] for d in (1,2,3)])
-    for a,(xq,yq) in enumerate(lines):
-        for b,zq in enumerate(zs):
-            send(FG.at[pl.ds(row0(lin(xq,yq,zq,1-c)),SL)],R.at[4*a+b],sib.at[4*a+b],pc)
-    U=176
-    def add(dst,d0,rows,srcs):
-        def body(t,_):
-            r=pl.multiple_of(t*U,16)
-            v=None
-            for s,s0 in srcs:
-                e=s[pl.ds(s0+r,U)].astype(jnp.float32); v=e if v is None else v+e
-            dst[pl.ds(d0+r,U)]=v.astype(dst.dtype)
-            return 0
-        lax.fori_loop(0,rows//U,body,0)
-    def have(k): wait(S.at[k],lsem.at[k]); wait(R.at[k],sib.at[k])
-    for b in range(4):
-        have(b)
-        add(S.at[b],0,SL,[(S.at[b],0),(R.at[b],0)])
-        send(S.at[b,pl.ds(0,half)],D0.at[b],dsem.at[0,b],py)
-        send(S.at[b,pl.ds(half,SL-half)],D1.at[b],dsem.at[1,b],px)
-    for b in range(4):
-        k=4+b; have(k); wait(D0.at[b],dsem.at[0,b])
-        add(S.at[k],0,half,[(S.at[k],0),(R.at[k],0),(D0.at[b],0)])
-        add(S.at[k],half,SL-half,[(S.at[k],half),(R.at[k],half)])
-        send(S.at[k],X.at[b],xsem.at[b],px)
-        k=8+b; have(k); wait(D1.at[b],dsem.at[1,b])
-        add(S.at[k],0,half,[(S.at[k],0),(R.at[k],0)])
-        add(S.at[k],half,SL-half,[(S.at[k],half),(R.at[k],half),(D1.at[b],0)])
-        send(S.at[k],Y.at[b],ysem.at[b],py)
-    for b in range(4):
-        k=12+b; have(k); wait(X.at[b],xsem.at[b]); wait(Y.at[b],ysem.at[b])
-        if b<3:
-            add(S.at[k],0,SL,[(S.at[k],0),(R.at[k],0),(X.at[b],0),(Y.at[b],0)])
-            send(S.at[k],Z.at[b],zsem.at[b],pz[b+1])
-    for b in range(3): wait(Z.at[b],zsem.at[b])
-    add(A,0,SL,[(S.at[15],0),(R.at[15],0),(X.at[3],0),(Y.at[3],0),(Z.at[0],0),(Z.at[1],0),(Z.at[2],0)])
-    start=me*p.sh; r_first=start//LN; s=start-r_first*LN; r0=r_first%16
-    A[0:SL]=pltpu.roll(A[0:SL],lax.rem(LN-s,LN),1)
-    lane=lax.broadcasted_iota(jnp.int32,(p.rows_in,LN),1)
-    out[...]=jnp.where(lane<LN-s,A[pl.ds(r0,p.rows_in),:],A[pl.ds(r0+1,p.rows_in),:])
-    for cp in pend: cp.wait_send()
-def scatter(p,FG):
-    SL=p.slot; half=SL//32*16; bf=jnp.bfloat16
-    DM=pltpu.SemaphoreType.DMA
-    o=pl.pallas_call(functools.partial(scatter_kernel,p),out_shape=jax.ShapeDtypeStruct((p.rows_in,LN),jnp.float32),
-        in_specs=[pl.BlockSpec(memory_space=pl.ANY)],
-        scratch_shapes=[pltpu.VMEM((16,SL,LN),bf),pltpu.VMEM((16,SL,LN),bf),pltpu.VMEM((4,half,LN),bf),pltpu.VMEM((4,SL-half,LN),bf),
-            pltpu.VMEM((4,SL,LN),bf),pltpu.VMEM((4,SL,LN),bf),pltpu.VMEM((3,SL,LN),bf),pltpu.VMEM((SL+32,LN),jnp.float32),
-            DM((16,)),DM((40,)),DM((16,)),DM((2,4)),DM((4,)),DM((4,)),DM((3,))],
-        compiler_params=pltpu.CompilerParams(collective_id=1,has_side_effects=True,vmem_limit_bytes=58<<20))(FG)
-    return o.reshape(-1)[:p.sh]
 
 def me_of():
     return lax.axis_index(AX)
@@ -568,7 +387,7 @@
     return None
 
 
-def weight_grad(r, lhs, rhs, base, rows, w, RB=256, CB=6):
+def weight_grad(r, lhs, rhs, base, rows, w, RB=256, CB=6, hook=None):
     lead = base % 16
     step_rows = RB * w
     F = r.F
@@ -597,6 +416,8 @@
         lax.fori_loop(0, step_rows // U, emit, 0)
         if lead:
             F[0:16] = F[step_rows : step_rows + 16]
+        if hook is not None:
+            hook(s)
         return 0
 
     lax.fori_loop(0, rows // RB, body, 0)
@@ -731,14 +552,643 @@
     )(length, tok, V, VG, qkv, lse, mixed, xh1, rstd1, first_low, act, gd, res, d_outer, wqkv, wo, w1, w2)
 
 
+class Gather:
+    def __init__(self, p, G, ssem, rsem, gosem):
+        self.p, self.G, self.ssem, self.rsem, self.gosem = p, G, ssem, rsem, gosem
+        self.x, self.y, self.z, self.c = coords()
+        x, y, z, c = self.x, self.y, self.z, self.c
+        self.me = lin(x, y, z, c)
+        half = p.slot // 32 * 16
+        self.H = ((0, half), (half, p.slot - half), (0, p.slot))
+        self.px, self.py, self.pc = dev(1 - x, y, z, c), dev(x, 1 - y, z, c), dev(x, y, z, 1 - c)
+
+    def enter(self):
+        x, y, z, c = self.x, self.y, self.z, self.c
+        bar = pltpu.get_barrier_semaphore()
+
+        def greet(to):
+            pl.semaphore_signal(bar, inc=1, device_id=to, device_id_type=MESH)
+
+        for to in (self.px, self.py, self.pc):
+            greet(to)
+        pl.when(z > 0)(lambda: greet(dev(x, y, z - 1, c)))
+        pl.when(z < 3)(lambda: greet(dev(x, y, z + 1, c)))
+        middle = (z > 0) & (z < 3)
+        pl.when(middle)(lambda: pl.semaphore_wait(bar, 5))
+        pl.when(jnp.logical_not(middle))(lambda: pl.semaphore_wait(bar, 4))
+
+    def send(self, sl, h, to, t):
+        r0, rn = self.H[h]
+        ref = self.G.at[sl, pl.ds(r0, rn)]
+        pltpu.make_async_remote_copy(src_ref=ref, dst_ref=ref, send_sem=self.ssem.at[sl, t], recv_sem=self.rsem.at[sl, h], device_id=to, device_id_type=MESH).start()
+
+    def wait(self, sl, h, sem=None):
+        r0, rn = self.H[h]
+        ref = self.G.at[sl, pl.ds(r0, rn)]
+        pltpu.make_async_copy(ref, ref, self.rsem.at[sl, h] if sem is None else sem).wait()
+
+    def up(self, sl):
+        pl.when(self.z < 3)(lambda: self.send(sl, 2, dev(self.x, self.y, self.z + 1, self.c), 3))
+
+    def down(self, sl):
+        pl.when(self.z > 0)(lambda: self.send(sl, 2, dev(self.x, self.y, self.z - 1, self.c), 4))
+
+    def core(self, sl, h=2):
+        self.send(sl, h, self.pc, 2)
+
+    def xy(self, sl):
+        self.send(sl, 2, self.px, 0)
+        self.send(sl, 2, self.py, 1)
+
+    def go(self, k):
+        pl.semaphore_signal(self.gosem.at[k], inc=1, device_id=self.pc, device_id_type=MESH)
+
+    def wait_go(self, k):
+        pl.semaphore_wait(self.gosem.at[k], 1)
+
+    def at(self, k, fn):
+        if k == 0:
+            fn(self.z)
+            return
+        pl.when(self.z - k >= 0)(lambda: fn(self.z - k))
+        pl.when(self.z + k <= 3)(lambda: fn(self.z + k))
+
+    def along_z(self, k, xy):
+        x, y, z, c = self.x, self.y, self.z, self.c
+
+        def below():
+            sl = lin(x, y, z - k, c)
+            self.wait(sl, 2)
+            self.up(sl)
+            if xy:
+                self.xy(sl)
+            self.core(sl)
+
+        def above():
+            sl = lin(x, y, z + k, c)
+            self.wait(sl, 2)
+            self.down(sl)
+            if xy:
+                self.xy(sl)
+            self.core(sl)
+
+        pl.when(z - k >= 0)(below)
+        pl.when(z + k <= 3)(above)
+
+    def sides(self, k):
+        x, y, c = self.x, self.y, self.c
+
+        def fn(zq):
+            sl = lin(1 - x, y, zq, c)
+            self.wait(sl, 2)
+            self.send(sl, 0, self.py, 1)
+            self.core(sl)
+            sl = lin(x, 1 - y, zq, c)
+            self.wait(sl, 2)
+            self.send(sl, 1, self.px, 0)
+            self.core(sl)
+
+        self.at(k, fn)
+
+    def diagonal(self, k):
+        def fn(zq):
+            sl = lin(1 - self.x, 1 - self.y, zq, self.c)
+            for h in (0, 1):
+                self.wait(sl, h)
+                self.core(sl, h)
+
+        self.at(k, fn)
+
+    def from_sibling(self, xp):
+        x, y, c = self.x, self.y, self.c
+
+        def body(zq, carry):
+            self.wait(lin(xp, y, zq, 1 - c), 2)
+            other = lin(xp, 1 - y, zq, 1 - c)
+            pl.when(x == xp)(lambda: self.wait(other, 2))
+
+            def halves():
+                self.wait(other, 0)
+                self.wait(other, 1)
+
+            pl.when(x != xp)(halves)
+            return carry
+
+        lax.fori_loop(0, 4, body, 0)
+
+    def leave(self):
+        x, y, z, c = self.x, self.y, self.z, self.c
+        W = self.wait
+
+        def body(zq, carry):
+            sl = lin(x, y, zq, c)
+            for t in (0, 1, 2):
+                W(sl, 2, self.ssem.at[sl, t])
+            pl.when((zq <= z) & (z < 3))(lambda: W(sl, 2, self.ssem.at[sl, 3]))
+            pl.when((zq >= z) & (z > 0))(lambda: W(sl, 2, self.ssem.at[sl, 4]))
+            sx = lin(1 - x, y, zq, c)
+            W(sx, 0, self.ssem.at[sx, 1])
+            W(sx, 2, self.ssem.at[sx, 2])
+            sy = lin(x, 1 - y, zq, c)
+            W(sy, 1, self.ssem.at[sy, 0])
+            W(sy, 2, self.ssem.at[sy, 2])
+            sd = lin(1 - x, 1 - y, zq, c)
+            W(sd, 2, self.ssem.at[sd, 2])
+            return carry
+
+        lax.fori_loop(0, 4, body, 0)
+
+
+FORWARD_OUT = ("hidden", "nested", "wqkv", "wo", "w1", "w2", "V", "VG", "qkv", "lse", "mixed", "xh1", "rstd1", "first_low", "act", "gd", "res", "d_outer")
+FORWARD_SHAPES = dict(
+    hidden=((LEN, D), jnp.bfloat16),
+    nested=((1, 1728), jnp.float32),
+    wqkv=((D, 3 * D), jnp.bfloat16),
+    wo=((D, D), jnp.bfloat16),
+    w1=((D, FF), jnp.bfloat16),
+    w2=((FF, D), jnp.bfloat16),
+    V=((16, FF), jnp.float32),
+    VG=((16, FF), jnp.float32),
+    qkv=((LEN, 3 * D), jnp.bfloat16),
+    lse=((LEN, LN), jnp.float32),
+    mixed=((LEN, D), jnp.bfloat16),
+    xh1=((LEN, D), jnp.float32),
+    rstd1=((LEN, 1), jnp.float32),
+    first_low=((LEN, D), jnp.bfloat16),
+    act=((LEN, FF), jnp.bfloat16),
+    gd=((LEN, FF), jnp.bfloat16),
+    res=((LEN, D), jnp.float32),
+    d_outer=((LEN, D), jnp.bfloat16),
+)
+
+
+def own_slot(p, me, x_ref, F, G):
+    start = me * p.sh
+    r_first = start // LN
+    s = start - r_first * LN
+    r0 = r_first % 16
+    lead = 32
+    F[0 : lead + p.slot + 32] = jnp.zeros((lead + p.slot + 32, LN), F32)
+    F[lead : lead + p.rows_in] = pltpu.roll(x_ref[...].astype(F32), s, 1)
+    lane = lax.broadcasted_iota(jnp.int32, (p.slot, LN), 1)
+    G[me] = jnp.where(lane >= s, F[pl.ds(lead - r0, p.slot), :], F[pl.ds(lead - 1 - r0, p.slot), :]).astype(BF)
+
+
+def relayout_vector(p, r, which):
+    at = sum(cnt for _, cnt in VECS[:which])
+    base, cnt = VECS[which]
+    g_lo = base // 16
+    load_flat(p, r.slots, r.F, g_lo, -(-(base + cnt) // 16), base + cnt)
+    for k in range(cnt):
+        name, j = vec_at(at + k)
+        f = base - 16 * g_lo + k
+        r.V[name : name + 1, j * LN : (j + 1) * LN] = r.F[f : f + 1]
+
+
+def relayout_rows(p, r, name, W, row, rows):
+    base, _, w = {n: (b, k, c) for n, b, k, c in MATS}[name]
+    lo = base + row * w
+    g_lo = lo // 16
+    load_flat(p, r.slots, r.F, g_lo, -(-(lo + rows * w) // 16), lo + rows * w)
+    tile_rows(r.F, W, lo - 16 * g_lo, row, rows, w)
+
+
+def gather_forward_kernel(p, x_ref, length, tok, hcot, ncot, *refs):
+    n = len(FORWARD_OUT)
+    outs = dict(zip(FORWARD_OUT, refs[:n]))
+    loc = dict(zip(FORWARD_OUT, refs[n : 2 * n]))
+    G, F, qb, xh2, rstd2, ssem, rsem, gosem, osem = refs[2 * n :]
+    r = Refs(slots=G, length=length[0], tok=tok, hcot=hcot, ncot=ncot, F=F, qb=qb, xh2=xh2, rstd2=rstd2, **loc)
+    g = Gather(p, G, ssem, rsem, gosem)
+    own_slot(p, g.me, x_ref, F, G)
+    g.enter()
+    c0, c1 = g.c == 0, g.c == 1
+
+    def first_planes():
+        g.up(g.me)
+        g.down(g.me)
+        g.xy(g.me)
+        g.core(g.me)
+        g.along_z(1, True)
+        g.sides(0)
+        g.along_z(2, True)
+        g.sides(1)
+        g.along_z(3, True)
+        g.go(0)
+        g.diagonal(0)
+        g.sides(2)
+        g.diagonal(1)
+        g.go(1)
+        g.sides(3)
+        g.diagonal(2)
+        g.diagonal(3)
+
+    def second_planes():
+        g.wait_go(0)
+        g.up(g.me)
+        g.down(g.me)
+        g.core(g.me)
+        for k in (1, 2, 3):
+            g.along_z(k, False)
+        g.wait_go(1)
+        for k in range(4):
+            g.at(k, lambda zq: g.xy(lin(g.x, g.y, zq, g.c)))
+        g.from_sibling(0)
+
+    pl.when(c0)(first_planes)
+    pl.when(c1)(second_planes)
+    started = []
+
+    def out(*names):
+        for m in names:
+            k = FORWARD_OUT.index(m)
+            cp = pltpu.make_async_copy(loc[m], outs[m], osem.at[k])
+            cp.start()
+            started.append(cp)
+
+    relayout_vector(p, r, 0)
+    for k in range(3):
+        relayout_rows(p, r, "wqkv", r.wqkv, 256 * k, 256)
+    out("wqkv")
+    forward_qkv(r)
+    out("qkv")
+    pl.when(c1)(lambda: g.sides(0))
+    r.lse[...] = jnp.zeros_like(r.lse)
+
+    def heads(hp, carry):
+        forward_heads(r, hp)
+        pl.when((hp == 1) & c1)(lambda: g.sides(1))
+        pl.when((hp == 3) & c1)(lambda: g.sides(2))
+        pl.when((hp == 4) & c1)(lambda: g.diagonal(0))
+        pl.when((hp == 5) & c1)(lambda: g.sides(3))
+        return carry
+
+    lax.fori_loop(0, H // 2, heads, 0)
+    out("lse", "mixed")
+    pl.when(c1)(lambda: g.from_sibling(1))
+    relayout_rows(p, r, "w1", r.w1, 448, 128)
+    relayout_rows(p, r, "w1", r.w1, 576, 192)
+    pl.when(c1)(lambda: g.diagonal(1))
+    relayout_rows(p, r, "w2", r.w2, 0, 768)
+    relayout_vector(p, r, 2)
+
+    def rest():
+        g.diagonal(2)
+        g.diagonal(3)
+
+    pl.when(c1)(rest)
+    pl.when(c0)(lambda: g.from_sibling(0))
+    relayout_rows(p, r, "wo", r.wo, 0, 768)
+    relayout_vector(p, r, 1)
+    out("wo")
+    forward_first(r)
+    out("xh1", "rstd1", "first_low")
+    relayout_rows(p, r, "w1", r.w1, 0, 256)
+    relayout_rows(p, r, "w1", r.w1, 256, 192)
+    out("w1")
+    lax.fori_loop(0, FF // 256, lambda j, c: (forward_up(r, j), c)[1], 0)
+    out("act", "gd")
+    pl.when(c0)(lambda: g.from_sibling(1))
+    for k in range(1, 4):
+        relayout_rows(p, r, "w2", r.w2, 768 * k, 768)
+    relayout_vector(p, r, 3)
+    out("w2", "V")
+    tot = forward_second(r)
+    out("hidden")
+    d_pool = head(r, tot)
+    out("nested")
+    backward_second(r, d_pool)
+    out("VG", "res", "d_outer")
+    g.leave()
+    for cp in started:
+        cp.wait()
+
+
+def gather_forward(p, shard, length, tok, hcot, ncot):
+    x = jnp.pad(shard, (0, p.rows_in * LN - p.sh)).reshape(p.rows_in, LN)
+    S = jax.ShapeDtypeStruct
+    vm = pl.BlockSpec(memory_space=pltpu.VMEM)
+    sm = pl.BlockSpec(memory_space=pltpu.SMEM)
+    hbm = pl.BlockSpec(memory_space=pl.ANY)
+    VM = pltpu.VMEM
+    DM = pltpu.SemaphoreType.DMA
+    shapes = [FORWARD_SHAPES[m] for m in FORWARD_OUT]
+    res = pl.pallas_call(
+        functools.partial(gather_forward_kernel, p),
+        out_shape=[S(*s) for s in shapes],
+        in_specs=[vm, sm, vm, vm, vm],
+        out_specs=[hbm] * len(shapes),
+        scratch_shapes=[VM(*s) for s in shapes]
+        + [VM((p.n, p.slot, LN), BF), VM((6144 + 32, LN), F32), VM((1, 3 * D), F32), VM((LEN, D), F32), VM((LEN, 1), F32)]
+        + [DM((p.n, 5)), DM((p.n, 3)), pltpu.SemaphoreType.REGULAR((2,)), DM((len(shapes),))],
+        compiler_params=pltpu.CompilerParams(collective_id=0, has_side_effects=True, vmem_limit_bytes=64 << 20),
+    )(x, length, tok, hcot, ncot)
+    return dict(zip(FORWARD_OUT, res))
+
+
+SCHEDULE = (
+    (2, 1, 0, "diag", 1, 2, 2),
+    (4, 1, 0, "diag", 1, 0, 2),
+    (7, 1, 1, "yline", 1, 2, 2),
+    (7, 1, 0, "xline", 1, 2, 2),
+    (9, 0, 0, "diag", 1, 2, 2),
+    (10, 1, 1, "diag", 0, 2, 2),
+    (11, 1, 0, "xline", 1, 0, 2),
+    (11, 1, 1, "diag", 0, 0, 2),
+    (11, 1, 1, "yline", 1, 0, 2),
+    (12, 0, 0, "diag", 1, 0, 2),
+    (12, 0, 0, "xline", 1, 2, 2),
+    (13, 1, 1, "xline", 0, 2, 2),
+    (14, 1, 1, "xline", 0, 0, 2),
+    (14, 1, 1, "own", 1, 2, 1),
+    (17, 1, 0, "yline", 0, 2, 2),
+    (18, 0, 1, "yline", 1, 2, 2),
+    (20, 0, 0, "yline", 0, 0, 2),
+    (20, 0, 1, "diag", 0, 0, 2),
+    (20, 0, 1, "xline", 0, 0, 2),
+    (20, 0, 1, "diag", 0, 2, 2),
+    (20, 0, 0, "xline", 1, 0, 2),
+    (20, 0, 0, "own", 0, 0, 2),
+    (20, 1, 0, "own", 0, 2, 1),
+    (21, 0, 1, "xline", 0, 2, 2),
+    (21, 0, 0, "yline", 0, 2, 2),
+    (21, 1, 0, "yline", 0, 0, 2),
+    (21, 0, 1, "yline", 1, 0, 2),
+    (21, 1, 0, "own", 0, 0, 2),
+    (21, 0, 0, "own", 0, 2, 1),
+    (21, 0, 1, "own", 1, 2, 1),
+    (22, 0, 1, "own", 1, 0, 2),
+    (22, 1, 1, "own", 1, 0, 2),
+)
+
+
+class Scatter:
+    def __init__(self, p, FG, R, D0, D1, X, Y, Z, A, sems):
+        self.p, self.FG, self.R, self.D0, self.D1, self.X, self.Y, self.Z, self.A = p, FG, R, D0, D1, X, Y, Z, A
+        self.sib_s, self.sib_r, self.d_s, self.d_r, self.x_s, self.x_r, self.y_s, self.y_r, self.z_s, self.z_r = sems
+        self.x, self.y, self.z, self.c = coords()
+        x, y, z, c = self.x, self.y, self.z, self.c
+        self.SL = p.slot
+        self.half = p.slot // 32 * 16
+        self.px, self.py, self.pc = dev(1 - x, y, z, c), dev(x, 1 - y, z, c), dev(x, y, z, 1 - c)
+
+    def zq(self, b):
+        d = lax.rem(b + 1, 4)
+        z = self.z
+        return lax.rem(z % 2 + d % 2, 2) + 2 * lax.rem(z // 2 + d // 2, 2)
+
+    def enter(self):
+        x, y, c = self.x, self.y, self.c
+        barrier([self.px, self.py, self.pc] + [dev(x, y, self.zq(b), c) for b in range(3)])
+
+    def row0(self, slot):
+        return pl.multiple_of((slot * self.p.sh) // LN // 16 * 16, 16)
+
+    def fg(self, slot):
+        return self.row0(slot)
+
+    def copy(self, src, dst, ssem, rsem, to):
+        return pltpu.make_async_remote_copy(src_ref=src, dst_ref=dst, send_sem=ssem, recv_sem=rsem, device_id=to, device_id_type=MESH)
+
+    def wait(self, ref, sem):
+        pltpu.make_async_copy(ref, ref, sem).wait()
+
+    def to_sibling(self, xp):
+        def body(k, _):
+            dp = 2 * xp + 1 - self.c
+            i = 8 * xp + k
+            self.copy(self.FG.at[pl.ds(self.row0(dp * 8 + k), self.SL)], self.R.at[i], self.sib_s.at[i], self.sib_r.at[i], self.pc).start()
+            return 0
+
+        lax.fori_loop(0, 8, body, 0)
+
+    def add(self, dst, d0, rows, srcs, U=176):
+        def body(t, _):
+            r = pl.multiple_of(t * U, 16)
+            v = None
+            for s, s0 in srcs:
+                e = s[pl.ds(s0 + r, U)].astype(F32)
+                v = e if v is None else v + e
+            dst[pl.ds(d0 + r, U)] = v.astype(dst.dtype)
+            return 0
+
+        lax.fori_loop(0, rows // U, body, 0)
+
+    def have(self, xp, yq, zq):
+        fs = zq * 2 + yq
+        i = 8 * xp + fs
+        self.wait(self.R.at[i], self.sib_r.at[i])
+        return i, self.row0((2 * xp + self.c) * 8 + fs)
+
+    def diag(self, xp, b):
+        i, g = self.have(xp, 1 - self.y, self.zq(b))
+        half, rest = self.half, self.SL - self.half
+        R = self.R.at[i]
+        self.add(R, 0, self.SL, [(self.FG, g), (R, 0)])
+        self.copy(R.at[pl.ds(0, half)], self.D0.at[b], self.d_s.at[0, b], self.d_r.at[0, b], self.py).start()
+        self.copy(R.at[pl.ds(half, rest)], self.D1.at[b], self.d_s.at[1, b], self.d_r.at[1, b], self.px).start()
+
+    def xline(self, xp, b):
+        i, g = self.have(xp, self.y, self.zq(b))
+        half, rest = self.half, self.SL - self.half
+        R = self.R.at[i]
+        self.wait(self.D0.at[b], self.d_r.at[0, b])
+        self.add(R, half, rest, [(self.FG, g + half), (R, half)])
+        self.add(R, 0, half, [(self.FG, g), (R, 0), (self.D0.at[b], 0)])
+        self.copy(R, self.X.at[b], self.x_s.at[b], self.x_r.at[b], self.px).start()
+
+    def yline(self, xp, b):
+        i, g = self.have(xp, 1 - self.y, self.zq(b))
+        half, rest = self.half, self.SL - self.half
+        R = self.R.at[i]
+        self.wait(self.D1.at[b], self.d_r.at[1, b])
+        self.add(R, 0, half, [(self.FG, g), (R, 0)])
+        self.add(R, half, rest, [(self.FG, g + half), (R, half), (self.D1.at[b], 0)])
+        self.copy(R, self.Y.at[b], self.y_s.at[b], self.y_r.at[b], self.py).start()
+
+    def own(self, xp, b):
+        i, g = self.have(xp, self.y, self.zq(b))
+        R = self.R.at[i]
+        self.wait(self.X.at[b], self.x_r.at[b])
+        self.wait(self.Y.at[b], self.y_r.at[b])
+        self.add(R, 0, self.SL, [(self.FG, g), (R, 0), (self.X.at[b], 0), (self.Y.at[b], 0)])
+        self.copy(R, self.Z.at[b], self.z_s.at[b], self.z_r.at[b], dev(self.x, self.y, self.zq(b), self.c)).start()
+
+    def last(self, xp, out):
+        p, SL, A = self.p, self.SL, self.A
+        i, g = self.have(xp, self.y, self.z)
+        self.wait(self.X.at[3], self.x_r.at[3])
+        self.wait(self.Y.at[3], self.y_r.at[3])
+        for b in range(3):
+            self.wait(self.Z.at[b], self.z_r.at[b])
+        self.add(A, 0, SL, [(self.FG, g), (self.R.at[i], 0), (self.X.at[3], 0), (self.Y.at[3], 0)] + [(self.Z.at[b], 0) for b in range(3)])
+        start = lin(self.x, self.y, self.z, self.c) * p.sh
+        r_first = start // LN
+        s = start - r_first * LN
+        r0 = r_first % 16
+        A[0:SL] = pltpu.roll(A[0:SL], lax.rem(LN - s, LN), 1)
+        lane = lax.broadcasted_iota(jnp.int32, (p.rows_in, LN), 1)
+        out[...] = jnp.where(lane < LN - s, A[pl.ds(r0, p.rows_in), :], A[pl.ds(r0 + 1, p.rows_in), :])
+
+    def after(self, part, index=None):
+        for c in (0, 1):
+            for x in (0, 1):
+                todo = [e for e in SCHEDULE if e[:3] == (part, c, x)]
+                if todo:
+                    here = (self.c == c) & (self.x == x)
+                    if index is not None:
+                        here = here & (index[0] == index[1])
+
+                    def run(todo=todo):
+                        for _, _, _, step, xp, b0, n in todo:
+                            lax.fori_loop(b0, b0 + n, lambda b, k: (getattr(self, step)(xp, b), k)[1], 0)
+
+                    pl.when(here)(run)
+
+    def leave(self):
+        for k in range(16):
+            self.wait(self.R.at[k], self.sib_s.at[k])
+        for b in range(4):
+            self.wait(self.D0.at[b], self.d_s.at[0, b])
+            self.wait(self.D1.at[b], self.d_s.at[1, b])
+            self.wait(self.X.at[b], self.x_s.at[b])
+            self.wait(self.Y.at[b], self.y_s.at[b])
+        for b in range(3):
+            self.wait(self.Z.at[b], self.z_s.at[b])
+
+
+BACK_IN = ("act", "d_outer", "w2", "gd", "first_low", "w1", "res", "xh1", "rstd1", "V", "VG", "mixed", "wo", "qkv", "lse", "tok")
+
+
+def backward_scatter_kernel(p, length, *refs):
+    n = len(BACK_IN)
+    src = dict(zip(BACK_IN, refs[:n]))
+    wqkv_in = refs[n]
+    igrad, out = refs[n + 1 : n + 3]
+    loc = dict(zip(BACK_IN, refs[n + 3 : 2 * n + 3]))
+    FG, F, E, R, D0, D1, X, Y, Z, A, lsem, osem, *sems = refs[2 * n + 3 :]
+    r = Refs(length=length[0], FG=FG, F=F, E=E, **loc)
+    r.dqkv, r.d_branch, r.d_mixed = r.act, r.first_low, r.d_outer
+    sc = Scatter(p, FG, R, D0, D1, X, Y, Z, A, sems)
+    mats = {m: (b, k, c) for m, b, k, c in MATS}
+    loads = {m: pltpu.make_async_copy(src[m], loc[m], lsem.at[k]) for k, m in enumerate(BACK_IN)}
+    for m in BACK_IN:
+        loads[m].start()
+
+    def need(*names):
+        for m in names:
+            loads[m].wait()
+
+    sc.enter()
+    c0, c1 = sc.c == 0, sc.c == 1
+    x0, x1 = sc.x == 0, sc.x == 1
+
+    def both(cond, fn):
+        pl.when(cond)(fn)
+
+    need("act", "d_outer", "VG")
+    weight_grad(r, r.act, r.d_outer, *mats["w2"])
+    edge_grads(r, 3)
+    both(c0, lambda: sc.to_sibling(1))
+    sc.after(1)
+    need("w2", "gd")
+
+    def act_part(j, carry):
+        backward_act(r, j)
+        for k in range(4):
+            sc.after(2 + k, (j, 3 * k + 2))
+        return carry
+
+    lax.fori_loop(0, FF // 256, act_part, 0)
+    q_loads = [pltpu.make_async_copy(wqkv_in.at[:, pl.ds(k * D, D)], r.w2.at[pl.ds(k * D, D)], lsem.at[n + k]) for k in range(3)]
+    for q in q_loads:
+        q.start()
+    need("first_low")
+    weight_grad(r, r.first_low, r.gd, *mats["w1"], hook=lambda i: [sc.after(6 + k, (i, k)) for k in range(2)])
+    edge_grads(r, 2)
+    both(c1, lambda: sc.to_sibling(1))
+    sc.after(8)
+    need("w1", "res", "xh1", "rstd1", "V")
+    backward_first(r)
+    sc.after(9)
+    need("mixed")
+    weight_grad(r, r.mixed, r.d_branch, *mats["wo"])
+    edge_grads(r, 1)
+    both(c0, lambda: sc.to_sibling(0))
+    sc.after(10)
+    need("wo")
+    backward_mixed(r)
+    sc.after(11)
+    need("qkv", "lse")
+
+    def heads(hp, carry):
+        backward_heads(r, hp)
+        for k in range(6):
+            sc.after(12 + k, (hp, k))
+        return carry
+
+    lax.fori_loop(0, H // 2, heads, 0)
+    need("tok")
+    weight_grad(r, r.tok, r.dqkv, *mats["wqkv"], hook=lambda i: [sc.after(18 + k, (i, k)) for k in range(2)])
+    edge_grads(r, 0)
+    both(c1, lambda: sc.to_sibling(0))
+    sc.after(20)
+    for q in q_loads:
+        q.wait()
+
+    def tokens(b, carry):
+        o = rows_of(b, 256)
+        v = r.res[o, :]
+        for part in range(3):
+            v = v + mm_nt(r.dqkv[o, part * D : (part + 1) * D], r.w2[part * D : (part + 1) * D, :])
+        r.res[o, :] = v
+        sc.after(21, (b, 0))
+        return carry
+
+    lax.fori_loop(0, LEN // 256, tokens, 0)
+    grad_out = pltpu.make_async_copy(r.res, igrad, osem)
+    grad_out.start()
+    sc.after(22)
+    both(x0, lambda: sc.last(0, out))
+    both(x1, lambda: sc.last(1, out))
+    sc.leave()
+    grad_out.wait()
+
+
+def backward_scatter(p, length, wqkv, **arrays):
+    S = jax.ShapeDtypeStruct
+    sm = pl.BlockSpec(memory_space=pltpu.SMEM)
+    hbm = pl.BlockSpec(memory_space=pl.ANY)
+    ins = [arrays[m] for m in BACK_IN]
+    SL = p.slot
+    half = SL // 32 * 16
+    VM = pltpu.VMEM
+    DM = pltpu.SemaphoreType.DMA
+    igrad, o = pl.pallas_call(
+        functools.partial(backward_scatter_kernel, p),
+        out_shape=[S((LEN, D), F32), S((p.rows_in, LN), F32)],
+        in_specs=[sm] + [hbm] * (len(ins) + 1),
+        out_specs=[hbm, pl.BlockSpec(memory_space=pltpu.VMEM)],
+        scratch_shapes=[VM(a.shape, a.dtype) for a in ins]
+        + [VM((flat_rows(p), LN), BF), VM((6144 + 32, LN), F32), VM((160, LN), F32), VM((16, SL, LN), BF), VM((4, half, LN), BF), VM((4, SL - half, LN), BF), VM((4, SL, LN), BF), VM((4, SL, LN), BF), VM((3, SL, LN), BF), VM((SL + 32, LN), F32)]
+        + [DM((len(ins) + 3,)), DM, DM((16,)), DM((16,)), DM((2, 4)), DM((2, 4)), DM((4,)), DM((4,)), DM((4,)), DM((4,)), DM((3,)), DM((3,))],
+        compiler_params=pltpu.CompilerParams(collective_id=1, has_side_effects=True, vmem_limit_bytes=64 << 20),
+    )(length, *ins, wqkv)
+    return igrad, o.reshape(-1)[: p.sh]
+
+
 def on_device(p, fast, tokens, lengths, weight_shards, hidden_cotangent, nested_cotangent):
-    slot = build_slot(p, weight_shards, me_of)
-    slots = gather(p, slot) if fast else lax.all_gather(slot, AX, axis=0)
     tok = tokens.reshape(LEN, D)
-    (hidden, nested, wqkv, wo, w1, w2, V, VG, qkv, lse, mixed, xh1, rstd1, first_low, act, gd, res, d_outer) = forward_local(p, slots, lengths, tok, hidden_cotangent.reshape(LEN, D), nested_cotangent)
-    igrad, flat = backward_local(p, lengths, tok, V, VG, qkv, lse, mixed, xh1, rstd1, first_low, act, gd, res, d_outer, wqkv, wo, w1, w2)
-    shards = scatter(p, flat) if fast else scatter_plain(p, flat)
-    return (hidden.reshape(1, LEN, D), nested, igrad.reshape(1, LEN, D), shards)
+    hcot = hidden_cotangent.reshape(LEN, D)
+    if fast:
+        f = gather_forward(p, weight_shards, lengths, tok, hcot, nested_cotangent)
+        igrad, shards = backward_scatter(p, lengths, tok=tok, **{m: f[m] for m in BACK_IN + ("wqkv",) if m != "tok"})
+    else:
+        slots = lax.all_gather(build_slot(p, weight_shards, me_of), AX, axis=0)
+        f = dict(zip(FORWARD_OUT, forward_local(p, slots, lengths, tok, hcot, nested_cotangent)))
+        igrad, flat = backward_local(p, lengths, tok, *[f[m] for m in FORWARD_OUT[6:] + FORWARD_OUT[2:6]])
+        shards = scatter_plain(p, flat)
+    return (f["hidden"].reshape(1, LEN, D), f["nested"], igrad.reshape(1, LEN, D), shards)
 
 
 def solution(mesh):

time: 281 us -> 210 us (0.75)
  the two profiles are of different devices: /device:TPU:11 before, /device:TPU:0 now
where the time goes in v1:
time: 210 us; the launch traced here: 209 us
  Pallas kernels  201 us (96%)
  local copies, waits for them, and re-layouts  7.43 us (4%)
    pallas_call x1, Pallas kernels, backward_scatter(): pl.pallas_call(functools.partial(backward_scatter_kernel, p), out_shape=[...  105 us
    pallas_call x1, Pallas kernels, gather_forward(): pl.pallas_call(functools.partial(gather_forward_kernel, p), out_shape=[S(...  96.1 us
    unnamed x8, local copies, waits for them, and re-layouts  5.62 us

profile of v1, /device:TPU:0, one launch (start us, length us, event | category | flops | bytes accessed | tf_op | source)
XLA Modules:
  0.0 209.5 jit_solution(7642039008172888694)
XLA Ops:
  1.3 1.8 pad_bitcast_fusion.x_ref
  3.1 96.1 %shard_map.84 = (bf16[512,768]{1,0:T(8,128)(2,1)}, f32[1,1728]{1,0:T(1,128)}, bf16[768,2304]{1,0:T(8,128)(2,1)}, bf16[768,768]{1,0:T(8,128)(2,1)}, bf16[768,3072...) custom-call(bf16[1731,128]{1,0:T(8,128)(2,1)} %pad_bitcast_fusion.x_, ...), custom_call_target="tpu_custom_call" | custom-call | tf_op jit(solution)/shard_map/pallas_call | solution.py:876
  99.2 104.6 %shard_map.85 = (f32[512,768]{1,0:T(8,128)}, f32[1731,128]{1,0:T(8,128)}) custom-call(s32[1]{0:T(128)S(6)} %copy.13.length, bf16[512,3072]{1,0:T(8,128)(2,1)} %get-tuple-element.26.refs_0_, bf16[512,768]{1,0:T(8,128)(2,1)} %get-tuple-element.27.refs_1_, bf16[3072,768]{1,0:T(8,128)(2,1)} %get-tuple-element.28.refs_2_, ...), custom_call_target="tpu_custom_call" | custom-call | tf_op jit(solution)/shard_map/pallas_call | solution.py:1167
  203.8 0.0 copy-start
  203.8 0.0 copy-start.1
  203.8 2.2 %copy.14 = bf16[1,512,768]{2,1,0:T(8,128)(2,1)} copy(bf16[1,512,768]{2,1,0:T(8,128)(2,1)} %bitcast.13) | data formatting | bytes 1572864
  206.1 1.3 copy.15
  207.3 0.0 copy-done
  207.3 1.1 copy.16
  208.5 0.0 copy-done.1
  208.5 1.0 copy.17
Async XLA Ops:
  203.8 3.5 %copy-start = (f32[512,768]{1,0:T(8,128)S(1)}, f32[512,768]{1,0:T(8,128)}, u32[]{:S(2)}) copy-start(f32[512,768]{1,0:T(8,128)} %get-tuple-element.42) | copy-start | bytes 4718596
  203.8 4.7 %copy-start.1 = (f32[1731,128]{1,0:T(8,128)S(1)}, f32[1731,128]{1,0:T(8,128)}, u32[]{:S(2)}) copy-start(f32[1731,128]{1,0:T(8,128)} %get-tuple-element.43) | copy-start | bytes 2658820

commit v2 on v1

--- a/solution.py
+++ b/solution.py
@@ -144,6 +144,7 @@
 )
 VI = {name: k for k, (name, _) in enumerate(VNAMES)}
 PREFIXES = (D, E2, E3, E4, E5)
+UP = 768
 
 
 def mm(a, b):
@@ -176,11 +177,11 @@
     r.qb[...] = bias
 
     def body(j, _):
-        o = pl.ds(pl.multiple_of(j * 256, 256), 256)
+        o = pl.ds(pl.multiple_of(j * D, D), D)
         r.qkv[:, o] = (mm(r.tok[...], r.wqkv[:, o]) + r.qb[:, o]).astype(BF)
         return 0
 
-    lax.fori_loop(0, 3 * D // 256, body, 0)
+    lax.fori_loop(0, 3, body, 0)
 
 
 def half_lanes(h):
@@ -232,7 +233,7 @@
 
 
 def forward_up(r, j):
-    o = pl.ds(pl.multiple_of(j * 256, 256), 256)
+    o = pl.ds(pl.multiple_of(j * UP, UP), UP)
     v = mm(r.first_low[...], r.w1[:, o]) + r.V[VI["up_bias"] : VI["up_bias"] + 1, o]
     cdf = 0.5 * (1.0 + lax.erf(v * SQ))
     r.act[:, o] = (v * cdf).astype(BF)
@@ -294,8 +295,8 @@
 
 def backward_second(r, d_pool):
     def body(b, c):
-        o = rows_of(b, 128)
-        t = lax.broadcasted_iota(jnp.int32, (128, 1), 0) + b * 128
+        o = rows_of(b, 256)
+        t = lax.broadcasted_iota(jnp.int32, (256, 1), 0) + b * 256
         dy = (r.hcot[o, :].astype(F32) + d_pool) * (t < r.length).astype(F32)
         xh = r.xh2[o, :]
         res = norm_back(dy, vrow(r.V, "second_gain"), xh, r.rstd2[o, :])
@@ -305,14 +306,14 @@
         return (c[0] + sum_rows(dy * xh), c[1] + sum_rows(dy), c[2] + sum_rows(low.astype(F32)))
 
     z = jnp.zeros((1, D), F32)
-    a, b, c = lax.fori_loop(0, LEN // 128, body, (z, z, z))
+    a, b, c = lax.fori_loop(0, LEN // 256, body, (z, z, z))
     put_grad(r, "second_gain", a)
     put_grad(r, "second_shift", b)
     put_grad(r, "down_bias", c)
 
 
 def backward_act(r, j):
-    o = pl.ds(pl.multiple_of(j * 256, 256), 256)
+    o = pl.ds(pl.multiple_of(j * UP, UP), UP)
     d = (mm_nt(r.d_outer[...], r.w2[o, :]) * r.gd[:, o].astype(F32)).astype(BF)
     r.gd[:, o] = d
     r.VG[VI["up_bias"] : VI["up_bias"] + 1, o] = sum_rows(d.astype(F32))
@@ -498,7 +499,7 @@
     relayout_matrix(p, r, "wo", wo, 768)
     forward_first(r)
     relayout_matrix(p, r, "w1", w1, 256)
-    lax.fori_loop(0, FF // 256, lambda j, c: (forward_up(r, j), c)[1], 0)
+    lax.fori_loop(0, FF // UP, lambda j, c: (forward_up(r, j), c)[1], 0)
     relayout_matrix(p, r, "w2", w2, 768)
     tot = forward_second(r)
     d_pool = head(r, tot)
@@ -524,9 +525,9 @@
     VG[...] = VG0[...]
     igrad[...] = res[...]
     mats = {n: (b, k, c) for n, b, k, c in MATS}
-    weight_grad(r, act, d_outer, *mats["w2"])
+    weight_grad(r, act, d_outer, *mats["w2"], RB=1024, CB=2)
     edge_grads(r, 3)
-    lax.fori_loop(0, FF // 256, lambda j, c: (backward_act(r, j), c)[1], 0)
+    lax.fori_loop(0, FF // UP, lambda j, c: (backward_act(r, j), c)[1], 0)
     weight_grad(r, first_low, gd, *mats["w1"])
     edge_grads(r, 2)
     backward_first(r)
@@ -599,6 +600,9 @@
     def xy(self, sl):
         self.send(sl, 2, self.px, 0)
         self.send(sl, 2, self.py, 1)
+
+    def own_line(self, k):
+        self.at(k, lambda zq: self.xy(lin(self.x, self.y, zq, self.c)))
 
     def go(self, k):
         pl.semaphore_signal(self.gosem.at[k], inc=1, device_id=self.pc, device_id_type=MESH)
@@ -764,7 +768,16 @@
     g.enter()
     c0, c1 = g.c == 0, g.c == 1
 
-    def first_planes():
+    started = []
+
+    def out(*names):
+        for m in names:
+            k = FORWARD_OUT.index(m)
+            cp = pltpu.make_async_copy(loc[m], outs[m], osem.at[k])
+            cp.start()
+            started.append(cp)
+
+    def part_rq_0():
         g.up(g.me)
         g.down(g.me)
         g.xy(g.me)
@@ -772,72 +785,80 @@
         g.along_z(1, True)
         g.sides(0)
         g.along_z(2, True)
+        g.go(0)
         g.sides(1)
+        g.go(1)
         g.along_z(3, True)
-        g.go(0)
+        g.sides(2)
+        g.sides(3)
         g.diagonal(0)
-        g.sides(2)
         g.diagonal(1)
-        g.go(1)
-        g.sides(3)
         g.diagonal(2)
         g.diagonal(3)
 
-    def second_planes():
+    pl.when(c0)(part_rq_0)
+    def part_rq_1():
         g.wait_go(0)
         g.up(g.me)
         g.down(g.me)
         g.core(g.me)
-        for k in (1, 2, 3):
-            g.along_z(k, False)
+        g.along_z(1, False)
+        g.along_z(2, False)
+        g.along_z(3, False)
         g.wait_go(1)
-        for k in range(4):
-            g.at(k, lambda zq: g.xy(lin(g.x, g.y, zq, g.c)))
+        g.own_line(0)
+        g.own_line(1)
+        g.own_line(2)
+        g.own_line(3)
         g.from_sibling(0)
 
-    pl.when(c0)(first_planes)
-    pl.when(c1)(second_planes)
-    started = []
-
-    def out(*names):
-        for m in names:
-            k = FORWARD_OUT.index(m)
-            cp = pltpu.make_async_copy(loc[m], outs[m], osem.at[k])
-            cp.start()
-            started.append(cp)
-
+    pl.when(c1)(part_rq_1)
     relayout_vector(p, r, 0)
     for k in range(3):
         relayout_rows(p, r, "wqkv", r.wqkv, 256 * k, 256)
     out("wqkv")
+    def part_qkv_1():
+        g.sides(0)
+
+    pl.when(c1)(part_qkv_1)
     forward_qkv(r)
     out("qkv")
-    pl.when(c1)(lambda: g.sides(0))
     r.lse[...] = jnp.zeros_like(r.lse)
 
     def heads(hp, carry):
+        def part_hd1_1():
+            g.sides(1)
+
+        pl.when((hp == 1) & c1)(part_hd1_1)
+        def part_hd3_1():
+            g.sides(2)
+
+        pl.when((hp == 3) & c1)(part_hd3_1)
+        def part_hd5_1():
+            g.diagonal(0)
+            g.sides(3)
+
+        pl.when((hp == 5) & c1)(part_hd5_1)
         forward_heads(r, hp)
-        pl.when((hp == 1) & c1)(lambda: g.sides(1))
-        pl.when((hp == 3) & c1)(lambda: g.sides(2))
-        pl.when((hp == 4) & c1)(lambda: g.diagonal(0))
-        pl.when((hp == 5) & c1)(lambda: g.sides(3))
         return carry
 
     lax.fori_loop(0, H // 2, heads, 0)
     out("lse", "mixed")
-    pl.when(c1)(lambda: g.from_sibling(1))
+    def part_rwo_0():
+        g.from_sibling(0)
+
+    pl.when(c0)(part_rwo_0)
+    def part_rwo_1():
+        g.diagonal(1)
+        g.diagonal(2)
+        g.diagonal(3)
+        g.from_sibling(1)
+
+    pl.when(c1)(part_rwo_1)
     relayout_rows(p, r, "w1", r.w1, 448, 128)
     relayout_rows(p, r, "w1", r.w1, 576, 192)
-    pl.when(c1)(lambda: g.diagonal(1))
     relayout_rows(p, r, "w2", r.w2, 0, 768)
     relayout_vector(p, r, 2)
-
-    def rest():
-        g.diagonal(2)
-        g.diagonal(3)
-
-    pl.when(c1)(rest)
-    pl.when(c0)(lambda: g.from_sibling(0))
     relayout_rows(p, r, "wo", r.wo, 0, 768)
     relayout_vector(p, r, 1)
     out("wo")
@@ -846,9 +867,12 @@
     relayout_rows(p, r, "w1", r.w1, 0, 256)
     relayout_rows(p, r, "w1", r.w1, 256, 192)
     out("w1")
-    lax.fori_loop(0, FF // 256, lambda j, c: (forward_up(r, j), c)[1], 0)
+    lax.fori_loop(0, FF // UP, lambda j, c: (forward_up(r, j), c)[1], 0)
     out("act", "gd")
-    pl.when(c0)(lambda: g.from_sibling(1))
+    def part_rw2b_0():
+        g.from_sibling(1)
+
+    pl.when(c0)(part_rw2b_0)
     for k in range(1, 4):
         relayout_rows(p, r, "w2", r.w2, 768 * k, 768)
     relayout_vector(p, r, 3)
@@ -1087,7 +1111,7 @@
         pl.when(cond)(fn)
 
     need("act", "d_outer", "VG")
-    weight_grad(r, r.act, r.d_outer, *mats["w2"])
+    weight_grad(r, r.act, r.d_outer, *mats["w2"], RB=1024, CB=2)
     edge_grads(r, 3)
     both(c0, lambda: sc.to_sibling(1))
     sc.after(1)
@@ -1096,10 +1120,10 @@
     def act_part(j, carry):
         backward_act(r, j)
         for k in range(4):
-            sc.after(2 + k, (j, 3 * k + 2))
+            sc.after(2 + k, (j, k))
         return carry
 
-    lax.fori_loop(0, FF // 256, act_part, 0)
+    lax.fori_loop(0, FF // UP, act_part, 0)
     q_loads = [pltpu.make_async_copy(wqkv_in.at[:, pl.ds(k * D, D)], r.w2.at[pl.ds(k * D, D)], lsem.at[n + k]) for k in range(3)]
     for q in q_loads:
         q.start()

time: 210 us -> 200 us (0.952)
  Pallas kernels: 201 us -> 191 us
    pallas_call x1, Pallas kernels: 105 us -> 99.7 us  [backward_scatter(): pl.pallas_call(functools.partial(backward_scatter_kernel, p), out_shape=[...]
    pallas_call x1, Pallas kernels: 96.1 us -> 91.2 us  [gather_forward(): pl.pallas_call(functools.partial(gather_forward_kernel, p), out_shape=[S(...]
where the time goes in v2:
time: 200 us
  Pallas kernels  191 us (96%)
  local copies, waits for them, and re-layouts  7.43 us (4%)
    pallas_call x1, Pallas kernels, backward_scatter(): pl.pallas_call(functools.partial(backward_scatter_kernel, p), out_shape=[...  99.7 us
    pallas_call x1, Pallas kernels, gather_forward(): pl.pallas_call(functools.partial(gather_forward_kernel, p), out_shape=[S(...  91.2 us
    unnamed x8, local copies, waits for them, and re-layouts  5.62 us

profile of v2, /device:TPU:0, one launch (start us, length us, event | category | flops | bytes accessed | tf_op | source)
XLA Modules:
  0.0 199.6 jit_solution(6386579360750649470)
XLA Ops:
  1.3 1.8 pad_bitcast_fusion.x_ref
  3.1 91.2 %shard_map.84 = (bf16[512,768]{1,0:T(8,128)(2,1)}, f32[1,1728]{1,0:T(1,128)}, bf16[768,2304]{1,0:T(8,128)(2,1)}, bf16[768,768]{1,0:T(8,128)(2,1)}, bf16[768,3072...) custom-call(bf16[1731,128]{1,0:T(8,128)(2,1)} %pad_bitcast_fusion.x_, ...), custom_call_target="tpu_custom_call" | custom-call | tf_op jit(solution)/shard_map/pallas_call | solution.py:900
  94.3 99.7 %shard_map.85 = (f32[512,768]{1,0:T(8,128)}, f32[1731,128]{1,0:T(8,128)}) custom-call(s32[1]{0:T(128)S(6)} %copy.13.length, bf16[512,3072]{1,0:T(8,128)(2,1)} %get-tuple-element.26.refs_0_, bf16[512,768]{1,0:T(8,128)(2,1)} %get-tuple-element.27.refs_1_, bf16[3072,768]{1,0:T(8,128)(2,1)} %get-tuple-element.28.refs_2_, ...), custom_call_target="tpu_custom_call" | custom-call | tf_op jit(solution)/shard_map/pallas_call | solution.py:1191
  194.0 0.0 copy-start
  194.0 0.0 copy-start.1
  194.0 2.2 %copy.14 = bf16[1,512,768]{2,1,0:T(8,128)(2,1)} copy(bf16[1,512,768]{2,1,0:T(8,128)(2,1)} %bitcast.13) | data formatting | bytes 1572864
  196.2 1.3 copy.15
  197.5 0.0 copy-done
  197.5 1.1 copy.16
  198.6 0.0 copy-done.1
  198.6 1.0 copy.17
Async XLA Ops:
  194.0 3.5 %copy-start = (f32[512,768]{1,0:T(8,128)S(1)}, f32[512,768]{1,0:T(8,128)}, u32[]{:S(2)}) copy-start(f32[512,768]{1,0:T(8,128)} %get-tuple-element.42) | copy-start | bytes 4718596
  194.0 4.7 %copy-start.1 = (f32[1731,128]{1,0:T(8,128)S(1)}, f32[1731,128]{1,0:T(8,128)}, u32[]{:S(2)}) copy-start(f32[1731,128]{1,0:T(8,128)} %get-tuple-element.43) | copy-start | bytes 2658820

commit v3 on v2

--- a/solution.py
+++ b/solution.py
@@ -219,7 +219,7 @@
 
 def forward_first(r):
     def body(b, _):
-        o = rows_of(b, 256)
+        o = rows_of(b, LEN)
         v = r.tok[o, :].astype(F32) + mm(r.mixed[o, :], r.wo[...]) + vrow(r.V, "out_bias")
         cen = v - mean_last(v)
         rstd = lax.rsqrt(mean_last(cen * cen) + EPS)
@@ -229,7 +229,7 @@
         r.first_low[o, :] = (xh * vrow(r.V, "first_gain") + vrow(r.V, "first_shift")).astype(BF)
         return 0
 
-    lax.fori_loop(0, LEN // 256, body, 0)
+    lax.fori_loop(0, 1, body, 0)
 
 
 def forward_up(r, j):
@@ -242,7 +242,7 @@
 
 def forward_second(r):
     def body(b, tot):
-        o = rows_of(b, 256)
+        o = rows_of(b, LEN)
         first = r.xh1[o, :] * vrow(r.V, "first_gain") + vrow(r.V, "first_shift")
         v = first + mm(r.act[o, :], r.w2[...]) + vrow(r.V, "down_bias")
         cen = v - mean_last(v)
@@ -250,12 +250,12 @@
         xh = cen * rstd
         r.xh2[o, :] = xh
         r.rstd2[o, :] = rstd
-        t = lax.broadcasted_iota(jnp.int32, (256, 1), 0) + b * 256
+        t = lax.broadcasted_iota(jnp.int32, (LEN, 1), 0)
         hid = (xh * vrow(r.V, "second_gain") + vrow(r.V, "second_shift")) * (t < r.length).astype(F32)
         r.hidden[o, :] = hid.astype(BF)
         return tot + sum_rows(hid)
 
-    return lax.fori_loop(0, LEN // 256, body, jnp.zeros((1, D), F32))
+    return lax.fori_loop(0, 1, body, jnp.zeros((1, D), F32))
 
 
 def head(r, tot):
@@ -295,8 +295,8 @@
 
 def backward_second(r, d_pool):
     def body(b, c):
-        o = rows_of(b, 256)
-        t = lax.broadcasted_iota(jnp.int32, (256, 1), 0) + b * 256
+        o = rows_of(b, LEN)
+        t = lax.broadcasted_iota(jnp.int32, (LEN, 1), 0)
         dy = (r.hcot[o, :].astype(F32) + d_pool) * (t < r.length).astype(F32)
         xh = r.xh2[o, :]
         res = norm_back(dy, vrow(r.V, "second_gain"), xh, r.rstd2[o, :])
@@ -306,7 +306,7 @@
         return (c[0] + sum_rows(dy * xh), c[1] + sum_rows(dy), c[2] + sum_rows(low.astype(F32)))
 
     z = jnp.zeros((1, D), F32)
-    a, b, c = lax.fori_loop(0, LEN // 256, body, (z, z, z))
+    a, b, c = lax.fori_loop(0, 1, body, (z, z, z))
     put_grad(r, "second_gain", a)
     put_grad(r, "second_shift", b)
     put_grad(r, "down_bias", c)
@@ -321,7 +321,7 @@
 
 def backward_first(r):
     def body(b, c):
-        o = rows_of(b, 256)
+        o = rows_of(b, LEN)
         dy = mm_nt(r.gd[o, :], r.w1[...]) + r.res[o, :]
         xh = r.xh1[o, :]
         res = norm_back(dy, vrow(r.V, "first_gain"), xh, r.rstd1[o, :])
@@ -331,7 +331,7 @@
         return (c[0] + sum_rows(dy * xh), c[1] + sum_rows(dy), c[2] + sum_rows(low.astype(F32)))
 
     z = jnp.zeros((1, D), F32)
-    a, b, c = lax.fori_loop(0, LEN // 256, body, (z, z, z))
+    a, b, c = lax.fori_loop(0, 1, body, (z, z, z))
     put_grad(r, "first_gain", a)
     put_grad(r, "first_shift", b)
     put_grad(r, "out_bias", c)
@@ -588,18 +588,29 @@
         ref = self.G.at[sl, pl.ds(r0, rn)]
         pltpu.make_async_copy(ref, ref, self.rsem.at[sl, h] if sem is None else sem).wait()
 
-    def up(self, sl):
-        pl.when(self.z < 3)(lambda: self.send(sl, 2, dev(self.x, self.y, self.z + 1, self.c), 3))
-
-    def down(self, sl):
-        pl.when(self.z > 0)(lambda: self.send(sl, 2, dev(self.x, self.y, self.z - 1, self.c), 4))
-
-    def core(self, sl, h=2):
+    def up(self, sl, h):
+        pl.when(self.z < 3)(lambda: self.send(sl, h, dev(self.x, self.y, self.z + 1, self.c), 3))
+
+    def down(self, sl, h):
+        pl.when(self.z > 0)(lambda: self.send(sl, h, dev(self.x, self.y, self.z - 1, self.c), 4))
+
+    def core(self, sl, h):
         self.send(sl, h, self.pc, 2)
 
     def xy(self, sl):
-        self.send(sl, 2, self.px, 0)
-        self.send(sl, 2, self.py, 1)
+        self.send(sl, 0, self.px, 0)
+        self.send(sl, 1, self.py, 1)
+        self.send(sl, 1, self.px, 0)
+        self.send(sl, 0, self.py, 1)
+
+    def own(self, xy):
+        for h in (0, 1):
+            self.up(self.me, h)
+            self.down(self.me, h)
+        if xy:
+            self.xy(self.me)
+        for h in (0, 1):
+            self.core(self.me, h)
 
     def own_line(self, k):
         self.at(k, lambda zq: self.xy(lin(self.x, self.y, zq, self.c)))
@@ -620,37 +631,49 @@
     def along_z(self, k, xy):
         x, y, z, c = self.x, self.y, self.z, self.c
 
-        def below():
-            sl = lin(x, y, z - k, c)
-            self.wait(sl, 2)
-            self.up(sl)
+        def from_level(zq, on):
+            sl = lin(x, y, zq, c)
+            self.wait(sl, 0)
+            on(sl, 0)
             if xy:
-                self.xy(sl)
-            self.core(sl)
-
-        def above():
-            sl = lin(x, y, z + k, c)
-            self.wait(sl, 2)
-            self.down(sl)
+                self.send(sl, 0, self.px, 0)
+            self.core(sl, 0)
+            self.wait(sl, 1)
+            on(sl, 1)
             if xy:
-                self.xy(sl)
-            self.core(sl)
-
-        pl.when(z - k >= 0)(below)
-        pl.when(z + k <= 3)(above)
+                self.send(sl, 1, self.py, 1)
+                self.send(sl, 1, self.px, 0)
+                self.send(sl, 0, self.py, 1)
+            self.core(sl, 1)
+
+        pl.when(z - k >= 0)(lambda: from_level(z - k, self.up))
+        pl.when(z + k <= 3)(lambda: from_level(z + k, self.down))
 
     def sides(self, k):
         x, y, c = self.x, self.y, self.c
 
         def fn(zq):
             sl = lin(1 - x, y, zq, c)
-            self.wait(sl, 2)
+            self.wait(sl, 0)
             self.send(sl, 0, self.py, 1)
-            self.core(sl)
+            self.core(sl, 0)
             sl = lin(x, 1 - y, zq, c)
-            self.wait(sl, 2)
+            self.wait(sl, 1)
             self.send(sl, 1, self.px, 0)
-            self.core(sl)
+            self.core(sl, 1)
+
+        self.at(k, fn)
+
+    def sides_rest(self, k):
+        x, y, c = self.x, self.y, self.c
+
+        def fn(zq):
+            sl = lin(1 - x, y, zq, c)
+            self.wait(sl, 1)
+            self.core(sl, 1)
+            sl = lin(x, 1 - y, zq, c)
+            self.wait(sl, 0)
+            self.core(sl, 0)
 
         self.at(k, fn)
 
@@ -664,21 +687,12 @@
         self.at(k, fn)
 
     def from_sibling(self, xp):
-        x, y, c = self.x, self.y, self.c
-
-        def body(zq, carry):
-            self.wait(lin(xp, y, zq, 1 - c), 2)
-            other = lin(xp, 1 - y, zq, 1 - c)
-            pl.when(x == xp)(lambda: self.wait(other, 2))
-
-            def halves():
-                self.wait(other, 0)
-                self.wait(other, 1)
-
-            pl.when(x != xp)(halves)
+        def body(fs, carry):
+            for h in (0, 1):
+                self.wait((2 * xp + 1 - self.c) * 8 + fs, h)
             return carry
 
-        lax.fori_loop(0, 4, body, 0)
+        lax.fori_loop(0, 8, body, 0)
 
     def leave(self):
         x, y, z, c = self.x, self.y, self.z, self.c
@@ -778,38 +792,40 @@
             started.append(cp)
 
     def part_rq_0():
-        g.up(g.me)
-        g.down(g.me)
-        g.xy(g.me)
-        g.core(g.me)
+        g.own(True)
+        g.sides(0)
+        g.go(0)
         g.along_z(1, True)
-        g.sides(0)
-        g.along_z(2, True)
-        g.go(0)
         g.sides(1)
         g.go(1)
+        g.along_z(2, True)
+        g.diagonal(0)
+        g.sides_rest(0)
+        g.sides(2)
         g.along_z(3, True)
-        g.sides(2)
         g.sides(3)
-        g.diagonal(0)
+        g.diagonal(3)
+        g.diagonal(2)
+        g.sides_rest(3)
         g.diagonal(1)
-        g.diagonal(2)
-        g.diagonal(3)
+        g.sides_rest(1)
+        g.sides_rest(2)
 
     pl.when(c0)(part_rq_0)
     def part_rq_1():
         g.wait_go(0)
-        g.up(g.me)
-        g.down(g.me)
-        g.core(g.me)
+        g.own(False)
+        g.wait_go(1)
+        g.own_line(0)
         g.along_z(1, False)
         g.along_z(2, False)
+        g.sides(0)
         g.along_z(3, False)
-        g.wait_go(1)
-        g.own_line(0)
+        g.own_line(3)
         g.own_line(1)
         g.own_line(2)
-        g.own_line(3)
+        g.sides(3)
+        g.sides_rest(3)
         g.from_sibling(0)
 
     pl.when(c1)(part_rq_1)
@@ -818,7 +834,11 @@
         relayout_rows(p, r, "wqkv", r.wqkv, 256 * k, 256)
     out("wqkv")
     def part_qkv_1():
-        g.sides(0)
+        g.sides(1)
+        g.diagonal(0)
+        g.sides(2)
+        g.from_sibling(1)
+        g.sides_rest(0)
 
     pl.when(c1)(part_qkv_1)
     forward_qkv(r)
@@ -827,16 +847,17 @@
 
     def heads(hp, carry):
         def part_hd1_1():
-            g.sides(1)
+            g.sides_rest(1)
+            g.sides_rest(2)
+            g.diagonal(3)
 
         pl.when((hp == 1) & c1)(part_hd1_1)
         def part_hd3_1():
-            g.sides(2)
+            g.diagonal(1)
 
         pl.when((hp == 3) & c1)(part_hd3_1)
         def part_hd5_1():
-            g.diagonal(0)
-            g.sides(3)
+            g.diagonal(2)
 
         pl.when((hp == 5) & c1)(part_hd5_1)
         forward_heads(r, hp)
@@ -844,21 +865,14 @@
 
     lax.fori_loop(0, H // 2, heads, 0)
     out("lse", "mixed")
-    def part_rwo_0():
-        g.from_sibling(0)
-
-    pl.when(c0)(part_rwo_0)
-    def part_rwo_1():
-        g.diagonal(1)
-        g.diagonal(2)
-        g.diagonal(3)
-        g.from_sibling(1)
-
-    pl.when(c1)(part_rwo_1)
     relayout_rows(p, r, "w1", r.w1, 448, 128)
     relayout_rows(p, r, "w1", r.w1, 576, 192)
     relayout_rows(p, r, "w2", r.w2, 0, 768)
     relayout_vector(p, r, 2)
+    def part_rwo_0():
+        g.from_sibling(0)
+
+    pl.when(c0)(part_rwo_0)
     relayout_rows(p, r, "wo", r.wo, 0, 768)
     relayout_vector(p, r, 1)
     out("wo")
@@ -867,12 +881,12 @@
     relayout_rows(p, r, "w1", r.w1, 0, 256)
     relayout_rows(p, r, "w1", r.w1, 256, 192)
     out("w1")
+    def part_up_0():
+        g.from_sibling(1)
+
+    pl.when(c0)(part_up_0)
     lax.fori_loop(0, FF // UP, lambda j, c: (forward_up(r, j), c)[1], 0)
     out("act", "gd")
-    def part_rw2b_0():
-        g.from_sibling(1)
-
-    pl.when(c0)(part_rw2b_0)
     for k in range(1, 4):
         relayout_rows(p, r, "w2", r.w2, 768 * k, 768)
     relayout_vector(p, r, 3)
@@ -904,7 +918,7 @@
         out_specs=[hbm] * len(shapes),
         scratch_shapes=[VM(*s) for s in shapes]
         + [VM((p.n, p.slot, LN), BF), VM((6144 + 32, LN), F32), VM((1, 3 * D), F32), VM((LEN, D), F32), VM((LEN, 1), F32)]
-        + [DM((p.n, 5)), DM((p.n, 3)), pltpu.SemaphoreType.REGULAR((2,)), DM((len(shapes),))],
+        + [DM((p.n, 5)), DM((p.n, 2)), pltpu.SemaphoreType.REGULAR((2,)), DM((len(shapes),))],
         compiler_params=pltpu.CompilerParams(collective_id=0, has_side_effects=True, vmem_limit_bytes=64 << 20),
     )(x, length, tok, hcot, ncot)
     return dict(zip(FORWARD_OUT, res))
@@ -1090,10 +1104,10 @@
     wqkv_in = refs[n]
     igrad, out = refs[n + 1 : n + 3]
     loc = dict(zip(BACK_IN, refs[n + 3 : 2 * n + 3]))
-    FG, F, E, R, D0, D1, X, Y, Z, A, lsem, osem, *sems = refs[2 * n + 3 :]
+    FG, F, E, R, D0, D1, X, Y, Z, lsem, osem, *sems = refs[2 * n + 3 :]
     r = Refs(length=length[0], FG=FG, F=F, E=E, **loc)
     r.dqkv, r.d_branch, r.d_mixed = r.act, r.first_low, r.d_outer
-    sc = Scatter(p, FG, R, D0, D1, X, Y, Z, A, sems)
+    sc = Scatter(p, FG, R, D0, D1, X, Y, Z, F, sems)
     mats = {m: (b, k, c) for m, b, k, c in MATS}
     loads = {m: pltpu.make_async_copy(src[m], loc[m], lsem.at[k]) for k, m in enumerate(BACK_IN)}
     for m in BACK_IN:
@@ -1161,7 +1175,7 @@
         q.wait()
 
     def tokens(b, carry):
-        o = rows_of(b, 256)
+        o = rows_of(b, LEN)
         v = r.res[o, :]
         for part in range(3):
             v = v + mm_nt(r.dqkv[o, part * D : (part + 1) * D], r.w2[part * D : (part + 1) * D, :])
@@ -1169,7 +1183,7 @@
         sc.after(21, (b, 0))
         return carry
 
-    lax.fori_loop(0, LEN // 256, tokens, 0)
+    lax.fori_loop(0, 1, tokens, 0)
     grad_out = pltpu.make_async_copy(r.res, igrad, osem)
     grad_out.start()
     sc.after(22)
@@ -1194,7 +1208,7 @@
         in_specs=[sm] + [hbm] * (len(ins) + 1),
         out_specs=[hbm, pl.BlockSpec(memory_space=pltpu.VMEM)],
         scratch_shapes=[VM(a.shape, a.dtype) for a in ins]
-        + [VM((flat_rows(p), LN), BF), VM((6144 + 32, LN), F32), VM((160, LN), F32), VM((16, SL, LN), BF), VM((4, half, LN), BF), VM((4, SL - half, LN), BF), VM((4, SL, LN), BF), VM((4, SL, LN), BF), VM((3, SL, LN), BF), VM((SL + 32, LN), F32)]
+        + [VM((flat_rows(p), LN), BF), VM((6144 + 32, LN), F32), VM((160, LN), F32), VM((16, SL, LN), BF), VM((4, half, LN), BF), VM((4, SL - half, LN), BF), VM((4, SL, LN), BF), VM((4, SL, LN), BF), VM((3, SL, LN), BF)]
         + [DM((len(ins) + 3,)), DM, DM((16,)), DM((16,)), DM((2, 4)), DM((2, 4)), DM((4,)), DM((4,)), DM((4,)), DM((4,)), DM((3,)), DM((3,))],
         compiler_params=pltpu.CompilerParams(collective_id=1, has_side_effects=True, vmem_limit_bytes=64 << 20),
     )(length, *ins, wqkv)

time: 200 us -> 195 us (0.975)
  Pallas kernels: 191 us -> 186 us
    pallas_call x1, Pallas kernels: 91.2 us -> 85.8 us  [gather_forward(): pl.pallas_call(functools.partial(gather_forward_kernel, p), out_shape=[S(...]
where the time goes in v3:
time: 195 us; the launch traced here: 194 us
  Pallas kernels  186 us (95%)
  local copies, waits for them, and re-layouts  7.43 us (4%)
    pallas_call x1, Pallas kernels, backward_scatter(): pl.pallas_call(functools.partial(backward_scatter_kernel, p), out_shape=[...  99.8 us
    pallas_call x1, Pallas kernels, gather_forward(): pl.pallas_call(functools.partial(gather_forward_kernel, p), out_shape=[S(...  85.8 us
    unnamed x8, local copies, waits for them, and re-layouts  5.62 us

profile of v3, /device:TPU:0, one launch (start us, length us, event | category | flops | bytes accessed | tf_op | source)
XLA Modules:
  0.0 194.4 jit_solution(1340319938777819694)
XLA Ops:
  1.3 1.8 pad_bitcast_fusion.x_ref
  3.1 85.8 %shard_map.84 = (bf16[512,768]{1,0:T(8,128)(2,1)}, f32[1,1728]{1,0:T(1,128)}, bf16[768,2304]{1,0:T(8,128)(2,1)}, bf16[768,768]{1,0:T(8,128)(2,1)}, bf16[768,3072...) custom-call(bf16[1731,128]{1,0:T(8,128)(2,1)} %pad_bitcast_fusion.x_, ...), custom_call_target="tpu_custom_call" | custom-call | tf_op jit(solution)/shard_map/pallas_call | solution.py:914
  88.9 99.8 %shard_map.85 = (f32[512,768]{1,0:T(8,128)}, f32[1731,128]{1,0:T(8,128)}) custom-call(s32[1]{0:T(128)S(6)} %copy.13.length, bf16[512,3072]{1,0:T(8,128)(2,1)} %get-tuple-element.26.refs_0_, bf16[512,768]{1,0:T(8,128)(2,1)} %get-tuple-element.27.refs_1_, bf16[3072,768]{1,0:T(8,128)(2,1)} %get-tuple-element.28.refs_2_, ...), custom_call_target="tpu_custom_call" | custom-call | tf_op jit(solution)/shard_map/pallas_call | solution.py:1205
  188.7 0.0 copy-start
  188.7 0.0 copy-start.1
  188.7 2.2 %copy.14 = bf16[1,512,768]{2,1,0:T(8,128)(2,1)} copy(bf16[1,512,768]{2,1,0:T(8,128)(2,1)} %bitcast.13) | data formatting | bytes 1572864
  190.9 1.3 copy.15
  192.2 0.0 copy-done
  192.2 1.1 copy.16
  193.4 0.0 copy-done.1
  193.4 1.0 copy.17
Async XLA Ops:
  188.7 3.5 %copy-start = (f32[512,768]{1,0:T(8,128)S(1)}, f32[512,768]{1,0:T(8,128)}, u32[]{:S(2)}) copy-start(f32[512,768]{1,0:T(8,128)} %get-tuple-element.42) | copy-start | bytes 4718596
  188.7 4.7 %copy-start.1 = (f32[1731,128]{1,0:T(8,128)S(1)}, f32[1731,128]{1,0:T(8,128)}, u32[]{:S(2)}) copy-start(f32[1731,128]{1,0:T(8,128)} %get-tuple-element.43) | copy-start | bytes 2658820

commit v4 on v3

--- a/solution.py
+++ b/solution.py
@@ -925,38 +925,62 @@
 
 
 SCHEDULE = (
-    (2, 1, 0, "diag", 1, 2, 2),
-    (4, 1, 0, "diag", 1, 0, 2),
-    (7, 1, 1, "yline", 1, 2, 2),
-    (7, 1, 0, "xline", 1, 2, 2),
-    (9, 0, 0, "diag", 1, 2, 2),
-    (10, 1, 1, "diag", 0, 2, 2),
-    (11, 1, 0, "xline", 1, 0, 2),
-    (11, 1, 1, "diag", 0, 0, 2),
-    (11, 1, 1, "yline", 1, 0, 2),
-    (12, 0, 0, "diag", 1, 0, 2),
-    (12, 0, 0, "xline", 1, 2, 2),
-    (13, 1, 1, "xline", 0, 2, 2),
-    (14, 1, 1, "xline", 0, 0, 2),
-    (14, 1, 1, "own", 1, 2, 1),
-    (17, 1, 0, "yline", 0, 2, 2),
-    (18, 0, 1, "yline", 1, 2, 2),
-    (20, 0, 0, "yline", 0, 0, 2),
+    (4, 1, 0, "diag", 1, 1, 2),
+    (7, 1, 0, "diag", 1, 3, 1),
+    (8, 1, 0, "xline", 1, 1, 1),
+    (9, 0, 0, "diag", 1, 0, 1),
+    (10, 0, 0, "diag", 1, 3, 1),
+    (10, 1, 0, "diag", 1, 0, 1),
+    (11, 0, 0, "diag", 1, 2, 1),
+    (11, 0, 1, "yline", 1, 0, 1),
+    (11, 1, 1, "yline", 1, 1, 1),
+    (11, 0, 0, "diag", 1, 1, 1),
+    (13, 1, 1, "diag", 0, 1, 1),
+    (14, 1, 1, "diag", 0, 2, 1),
+    (14, 1, 0, "yline", 0, 1, 1),
+    (14, 0, 0, "xline", 1, 0, 1),
+    (14, 1, 1, "diag", 0, 0, 1),
+    (15, 0, 1, "yline", 1, 1, 1),
+    (15, 1, 1, "own", 1, 1, 1),
+    (16, 1, 1, "xline", 0, 1, 1),
+    (16, 1, 0, "yline", 0, 2, 1),
+    (16, 0, 0, "xline", 1, 1, 1),
+    (17, 0, 0, "xline", 1, 3, 1),
+    (17, 1, 1, "xline", 0, 2, 1),
+    (17, 1, 1, "diag", 0, 3, 1),
+    (18, 1, 0, "own", 0, 1, 1),
+    (18, 1, 1, "yline", 1, 2, 1),
+    (19, 1, 0, "yline", 0, 0, 1),
+    (19, 1, 1, "xline", 0, 0, 1),
+    (19, 0, 0, "xline", 1, 2, 1),
+    (20, 0, 0, "yline", 0, 1, 2),
     (20, 0, 1, "diag", 0, 0, 2),
-    (20, 0, 1, "xline", 0, 0, 2),
-    (20, 0, 1, "diag", 0, 2, 2),
-    (20, 0, 0, "xline", 1, 0, 2),
-    (20, 0, 0, "own", 0, 0, 2),
+    (20, 1, 1, "own", 1, 2, 1),
     (20, 1, 0, "own", 0, 2, 1),
-    (21, 0, 1, "xline", 0, 2, 2),
-    (21, 0, 0, "yline", 0, 2, 2),
-    (21, 1, 0, "yline", 0, 0, 2),
-    (21, 0, 1, "yline", 1, 0, 2),
-    (21, 1, 0, "own", 0, 0, 2),
+    (20, 0, 1, "yline", 1, 2, 1),
+    (21, 0, 1, "diag", 0, 2, 1),
+    (21, 1, 1, "yline", 1, 0, 1),
+    (21, 0, 0, "own", 0, 1, 1),
+    (21, 0, 1, "own", 1, 1, 1),
+    (21, 0, 0, "yline", 0, 0, 1),
     (21, 0, 0, "own", 0, 2, 1),
-    (21, 0, 1, "own", 1, 2, 1),
-    (22, 0, 1, "own", 1, 0, 2),
-    (22, 1, 1, "own", 1, 0, 2),
+    (21, 0, 1, "xline", 0, 1, 1),
+    (21, 0, 1, "own", 1, 0, 1),
+    (22, 0, 1, "yline", 1, 3, 1),
+    (22, 1, 1, "own", 1, 0, 1),
+    (22, 1, 0, "yline", 0, 3, 1),
+    (22, 1, 0, "xline", 1, 0, 1),
+    (22, 0, 1, "xline", 0, 0, 1),
+    (22, 0, 1, "own", 1, 2, 1),
+    (22, 0, 1, "xline", 0, 2, 1),
+    (22, 0, 0, "own", 0, 0, 1),
+    (22, 0, 1, "diag", 0, 3, 1),
+    (22, 0, 0, "yline", 0, 3, 1),
+    (22, 0, 1, "xline", 0, 3, 1),
+    (22, 1, 0, "own", 0, 0, 1),
+    (22, 1, 0, "xline", 1, 2, 2),
+    (22, 1, 1, "xline", 0, 3, 1),
+    (22, 1, 1, "yline", 1, 3, 1),
 )
 
 
@@ -1212,7 +1236,26 @@
         + [DM((len(ins) + 3,)), DM, DM((16,)), DM((16,)), DM((2, 4)), DM((2, 4)), DM((4,)), DM((4,)), DM((4,)), DM((4,)), DM((3,)), DM((3,))],
         compiler_params=pltpu.CompilerParams(collective_id=1, has_side_effects=True, vmem_limit_bytes=64 << 20),
     )(length, *ins, wqkv)
-    return igrad, o.reshape(-1)[: p.sh]
+    return igrad, o
+
+
+def finish_copies(p, shards, hidden, igrad, nested):
+    S = jax.ShapeDtypeStruct
+    vm = pl.BlockSpec(memory_space=pltpu.VMEM)
+
+    def kernel(a, b, c, d, a_out, b_out, c_out, d_out):
+        a_out[...] = a[...].reshape(p.rows_in * LN)[: p.sh]
+        b_out[...] = b[...]
+        c_out[...] = c[...]
+        d_out[...] = d[...]
+
+    arrays = (shards, hidden, igrad, nested)
+    return pl.pallas_call(
+        kernel,
+        out_shape=[S((p.sh,), F32)] + [S(a.shape, a.dtype) for a in arrays[1:]],
+        in_specs=[vm] * 4,
+        out_specs=[vm] * 4,
+    )(*arrays)
 
 
 def on_device(p, fast, tokens, lengths, weight_shards, hidden_cotangent, nested_cotangent):
@@ -1221,6 +1264,7 @@
     if fast:
         f = gather_forward(p, weight_shards, lengths, tok, hcot, nested_cotangent)
         igrad, shards = backward_scatter(p, lengths, tok=tok, **{m: f[m] for m in BACK_IN + ("wqkv",) if m != "tok"})
+        shards, f["hidden"], igrad, f["nested"] = finish_copies(p, shards, f["hidden"], igrad, f["nested"])
     else:
         slots = lax.all_gather(build_slot(p, weight_shards, me_of), AX, axis=0)
         f = dict(zip(FORWARD_OUT, forward_local(p, slots, lengths, tok, hcot, nested_cotangent)))

time: 195 us -> 191 us (0.979)
  local copies, waits for them, and re-layouts: 7.43 us -> 1.81 us
  Pallas kernels: 186 us -> 188 us
    unnamed x8 -> x0, local copies, waits for them, and re-layouts: 5.62 us -> none
    pallas_call x0 -> x1, Pallas kernels: none -> 3.93 us  [finish_copies(): pl.pallas_call(kernel, out_shape=[S((p.sh,), F32)] + [S(a.shape, a.dtype)...]
where the time goes in v4:
time: 191 us
  Pallas kernels  188 us (98%)
    pallas_call x1, Pallas kernels, backward_scatter(): pl.pallas_call(functools.partial(backward_scatter_kernel, p), out_shape=[...  98.3 us
    pallas_call x1, Pallas kernels, gather_forward(): pl.pallas_call(functools.partial(gather_forward_kernel, p), out_shape=[S(...  85.8 us
    pallas_call x1, Pallas kernels, finish_copies(): pl.pallas_call(kernel, out_shape=[S((p.sh,), F32)] + [S(a.shape, a.dtype)...  3.93 us

profile of v4, /device:TPU:0, one launch (start us, length us, event | category | flops | bytes accessed | tf_op | source)
XLA Modules:
  0.0 191.1 jit_solution(3686363512202643808)
XLA Ops:
  1.3 1.8 pad_bitcast_fusion.x_ref
  3.1 85.8 %shard_map.84 = (bf16[512,768]{1,0:T(8,128)(2,1)}, f32[1,1728]{1,0:T(1,128)}, bf16[768,2304]{1,0:T(8,128)(2,1)}, bf16[768,768]{1,0:T(8,128)(2,1)}, bf16[768,3072...) custom-call(bf16[1731,128]{1,0:T(8,128)(2,1)} %pad_bitcast_fusion.x_, ...), custom_call_target="tpu_custom_call" | custom-call | tf_op jit(solution)/shard_map/pallas_call | solution.py:914
  88.9 98.3 %shard_map.85 = (f32[512,768]{1,0:T(8,128)}, f32[1731,128]{1,0:T(8,128)}) custom-call(s32[1]{0:T(128)S(6)} %copy.9.length, bf16[512,3072]{1,0:T(8,128)(2,1)} %get-tuple-element.28.refs_0_, bf16[512,768]{1,0:T(8,128)(2,1)} %get-tuple-element.29.refs_1_, bf16[3072,768]{1,0:T(8,128)(2,1)} %get-tuple-element.30.refs_2_, ...), custom_call_target="tpu_custom_call" | custom-call | tf_op jit(solution)/shard_map/pallas_call | solution.py:1229
  187.2 3.9 %shard_map.86 = (f32[221520]{0:T(1024)}, bf16[512,768]{1,0:T(8,128)(2,1)}, f32[512,768]{1,0:T(8,128)}, f32[1,1728]{1,0:T(1,128)}) custom-call(f32[1731,128]{1,0:T(8,128)} %get-tuple-element.44.a, bf16[512,768]{1,0:T(8,128)(2,1)} %get-tuple-element.45.b, f32[512,768]{1,0:T(8,128)} %get-tuple-element.46.c, f32[1,1728]{1,0:T(1,128)} %get-tuple-element.47.d), custom_call_target="tpu_custom_call" | custom-call | tf_op jit(solution)/shard_map/pallas_call | solution.py:1253

commit v5 on v4

--- a/solution.py
+++ b/solution.py
@@ -144,6 +144,7 @@
 )
 VI = {name: k for k, (name, _) in enumerate(VNAMES)}
 PREFIXES = (D, E2, E3, E4, E5)
+SCALE = 1.0 / math.sqrt(HD)
 UP = 768
 
 
@@ -194,14 +195,14 @@
 
 
 def forward_heads(r, hp):
-    q, k, v = pair(r, 0, hp), pair(r, 1, hp), pair(r, 2, hp)
+    q, k, v = pair(r, 0, hp) * SCALE, pair(r, 1, hp), pair(r, 2, hp)
     valid = lax.broadcasted_iota(jnp.int32, (1, LEN), 1) < r.length
     out = None
     lse_all = r.lse[...]
     lane = lax.broadcasted_iota(jnp.int32, (LEN, LN), 1)
     for h in range(2):
         qh = jnp.where(half_lanes(h), q, jnp.zeros_like(q))
-        s = jnp.where(valid, mm_nt(qh, k) * 0.125, -1e9)
+        s = jnp.where(valid, mm_nt(qh, k), -1e9)
         m = jnp.max(s, axis=1, keepdims=True)
         e = jnp.exp(s - m)
         l = jnp.sum(e, axis=1, keepdims=True)
@@ -342,24 +343,27 @@
 
 
 def backward_heads(r, hp):
-    q, k, v = pair(r, 0, hp), pair(r, 1, hp), pair(r, 2, hp)
+    q, k, v = pair(r, 0, hp) * SCALE, pair(r, 1, hp), pair(r, 2, hp)
+    k_scaled = k * SCALE
     cols = pl.ds(pl.multiple_of(hp * LN, LN), LN)
     dm = r.d_mixed[:, cols]
     valid = lax.broadcasted_iota(jnp.int32, (1, LEN), 1) < r.length
     lane = lax.broadcasted_iota(jnp.int32, (LEN, LN), 1)
     zero = jnp.zeros_like(q)
+    dm_mixed = dm.astype(F32) * r.mixed[:, cols].astype(F32)
     dq = dk = dv = None
     for h in range(2):
         here = half_lanes(h)
-        qh, kh, dmh = jnp.where(here, q, zero), jnp.where(here, k, zero), jnp.where(here, dm, zero)
+        qh, kh, dmh = jnp.where(here, q, zero), jnp.where(here, k_scaled, zero), jnp.where(here, dm, zero)
         lse = jnp.sum(jnp.where(lane == 2 * hp + h, r.lse[...], 0.0), axis=1, keepdims=True)
-        s = jnp.where(valid, mm_nt(qh, k) * 0.125, -1e9)
+        s = jnp.where(valid, mm_nt(qh, k), -1e9)
         p = jnp.exp(s - lse)
         dp = mm_nt(dmh, v)
-        ds = (p * (dp - jnp.sum(dp * p, axis=1, keepdims=True))).astype(BF)
+        delta = jnp.sum(jnp.where(here, dm_mixed, 0.0), axis=1, keepdims=True)
+        ds = (p * (dp - delta)).astype(BF)
         a, b, c = mm(ds, kh), mm_tn(ds, qh), mm_tn(p.astype(BF), dmh)
         dq, dk, dv = (a, b, c) if dq is None else (dq + a, dk + b, dv + c)
-    dq, dk, dv = (dq * 0.125).astype(BF), (dk * 0.125).astype(BF), dv.astype(BF)
+    dq, dk, dv = dq.astype(BF), dk.astype(BF), dv.astype(BF)
     for part, g in ((0, dq), (1, dk), (2, dv)):
         r.dqkv[:, pl.ds(pl.multiple_of(part * D + hp * LN, LN), LN)] = g
     k = VI["q_bias"]
@@ -797,19 +801,19 @@
         g.go(0)
         g.along_z(1, True)
         g.sides(1)
+        g.sides_rest(0)
+        g.diagonal(0)
         g.go(1)
         g.along_z(2, True)
-        g.diagonal(0)
-        g.sides_rest(0)
         g.sides(2)
         g.along_z(3, True)
-        g.sides(3)
-        g.diagonal(3)
-        g.diagonal(2)
-        g.sides_rest(3)
         g.diagonal(1)
         g.sides_rest(1)
+        g.sides(3)
+        g.sides_rest(3)
+        g.diagonal(2)
         g.sides_rest(2)
+        g.diagonal(3)
 
     pl.when(c0)(part_rq_0)
     def part_rq_1():
@@ -818,15 +822,16 @@
         g.wait_go(1)
         g.own_line(0)
         g.along_z(1, False)
+        g.sides(0)
         g.along_z(2, False)
-        g.sides(0)
+        g.own_line(1)
         g.along_z(3, False)
         g.own_line(3)
-        g.own_line(1)
         g.own_line(2)
+        g.from_sibling(0)
         g.sides(3)
-        g.sides_rest(3)
-        g.from_sibling(0)
+        g.sides_rest(0)
+        g.diagonal(0)
 
     pl.when(c1)(part_rq_1)
     relayout_vector(p, r, 0)
@@ -834,11 +839,8 @@
         relayout_rows(p, r, "wqkv", r.wqkv, 256 * k, 256)
     out("wqkv")
     def part_qkv_1():
+        g.from_sibling(1)
         g.sides(1)
-        g.diagonal(0)
-        g.sides(2)
-        g.from_sibling(1)
-        g.sides_rest(0)
 
     pl.when(c1)(part_qkv_1)
     forward_qkv(r)
@@ -846,18 +848,19 @@
     r.lse[...] = jnp.zeros_like(r.lse)
 
     def heads(hp, carry):
-        def part_hd1_1():
+        def part_hd0_1():
             g.sides_rest(1)
+            g.sides(2)
+            g.sides_rest(3)
+
+        pl.when((hp == 0) & c1)(part_hd0_1)
+        def part_hd3_1():
             g.sides_rest(2)
             g.diagonal(3)
 
-        pl.when((hp == 1) & c1)(part_hd1_1)
-        def part_hd3_1():
-            g.diagonal(1)
-
         pl.when((hp == 3) & c1)(part_hd3_1)
         def part_hd5_1():
-            g.diagonal(2)
+            g.diagonal(1)
 
         pl.when((hp == 5) & c1)(part_hd5_1)
         forward_heads(r, hp)
@@ -865,6 +868,10 @@
 
     lax.fori_loop(0, H // 2, heads, 0)
     out("lse", "mixed")
+    def part_rw1b_1():
+        g.diagonal(2)
+
+    pl.when(c1)(part_rw1b_1)
     relayout_rows(p, r, "w1", r.w1, 448, 128)
     relayout_rows(p, r, "w1", r.w1, 576, 192)
     relayout_rows(p, r, "w2", r.w2, 0, 768)
@@ -878,13 +885,13 @@
     out("wo")
     forward_first(r)
     out("xh1", "rstd1", "first_low")
+    def part_rw1a_0():
+        g.from_sibling(1)
+
+    pl.when(c0)(part_rw1a_0)
     relayout_rows(p, r, "w1", r.w1, 0, 256)
     relayout_rows(p, r, "w1", r.w1, 256, 192)
     out("w1")
-    def part_up_0():
-        g.from_sibling(1)
-
-    pl.when(c0)(part_up_0)
     lax.fori_loop(0, FF // UP, lambda j, c: (forward_up(r, j), c)[1], 0)
     out("act", "gd")
     for k in range(1, 4):
@@ -925,60 +932,62 @@
 
 
 SCHEDULE = (
-    (4, 1, 0, "diag", 1, 1, 2),
-    (7, 1, 0, "diag", 1, 3, 1),
+    (4, 1, 0, "diag", 1, 2, 1),
+    (5, 1, 0, "diag", 1, 1, 1),
+    (8, 1, 1, "yline", 1, 2, 1),
     (8, 1, 0, "xline", 1, 1, 1),
-    (9, 0, 0, "diag", 1, 0, 1),
-    (10, 0, 0, "diag", 1, 3, 1),
-    (10, 1, 0, "diag", 1, 0, 1),
-    (11, 0, 0, "diag", 1, 2, 1),
-    (11, 0, 1, "yline", 1, 0, 1),
-    (11, 1, 1, "yline", 1, 1, 1),
-    (11, 0, 0, "diag", 1, 1, 1),
+    (10, 1, 1, "yline", 1, 1, 1),
+    (10, 1, 0, "diag", 1, 3, 1),
+    (10, 0, 0, "diag", 1, 0, 1),
+    (11, 0, 0, "diag", 1, 2, 2),
+    (12, 1, 1, "diag", 0, 0, 1),
+    (12, 0, 0, "diag", 1, 1, 1),
+    (13, 1, 1, "diag", 0, 2, 1),
     (13, 1, 1, "diag", 0, 1, 1),
-    (14, 1, 1, "diag", 0, 2, 1),
-    (14, 1, 0, "yline", 0, 1, 1),
-    (14, 0, 0, "xline", 1, 0, 1),
-    (14, 1, 1, "diag", 0, 0, 1),
-    (15, 0, 1, "yline", 1, 1, 1),
-    (15, 1, 1, "own", 1, 1, 1),
-    (16, 1, 1, "xline", 0, 1, 1),
-    (16, 1, 0, "yline", 0, 2, 1),
+    (13, 1, 0, "yline", 0, 2, 1),
+    (14, 1, 1, "diag", 0, 3, 1),
+    (14, 0, 0, "xline", 1, 2, 1),
+    (15, 0, 1, "yline", 1, 3, 1),
+    (16, 1, 1, "xline", 0, 2, 1),
     (16, 0, 0, "xline", 1, 1, 1),
-    (17, 0, 0, "xline", 1, 3, 1),
-    (17, 1, 1, "xline", 0, 2, 1),
-    (17, 1, 1, "diag", 0, 3, 1),
-    (18, 1, 0, "own", 0, 1, 1),
-    (18, 1, 1, "yline", 1, 2, 1),
-    (19, 1, 0, "yline", 0, 0, 1),
+    (16, 1, 0, "yline", 0, 1, 1),
+    (17, 1, 1, "own", 1, 1, 1),
+    (17, 0, 1, "yline", 1, 2, 1),
+    (18, 0, 0, "xline", 1, 0, 1),
+    (18, 0, 1, "yline", 1, 1, 1),
+    (18, 1, 1, "xline", 0, 1, 1),
+    (18, 1, 0, "yline", 0, 3, 1),
+    (19, 1, 0, "own", 0, 2, 1),
     (19, 1, 1, "xline", 0, 0, 1),
-    (19, 0, 0, "xline", 1, 2, 1),
-    (20, 0, 0, "yline", 0, 1, 2),
-    (20, 0, 1, "diag", 0, 0, 2),
-    (20, 1, 1, "own", 1, 2, 1),
-    (20, 1, 0, "own", 0, 2, 1),
-    (20, 0, 1, "yline", 1, 2, 1),
-    (21, 0, 1, "diag", 0, 2, 1),
+    (20, 0, 0, "yline", 0, 1, 1),
+    (20, 0, 1, "diag", 0, 1, 2),
+    (20, 0, 0, "yline", 0, 0, 1),
+    (20, 0, 1, "own", 1, 2, 1),
+    (20, 1, 0, "xline", 1, 2, 1),
     (21, 1, 1, "yline", 1, 0, 1),
+    (21, 0, 1, "diag", 0, 0, 1),
+    (21, 0, 1, "own", 1, 1, 1),
+    (21, 1, 0, "diag", 1, 0, 1),
     (21, 0, 0, "own", 0, 1, 1),
-    (21, 0, 1, "own", 1, 1, 1),
-    (21, 0, 0, "yline", 0, 0, 1),
-    (21, 0, 0, "own", 0, 2, 1),
-    (21, 0, 1, "xline", 0, 1, 1),
-    (21, 0, 1, "own", 1, 0, 1),
-    (22, 0, 1, "yline", 1, 3, 1),
+    (21, 1, 0, "xline", 1, 3, 1),
+    (22, 1, 0, "yline", 0, 0, 1),
+    (22, 1, 0, "own", 0, 1, 1),
+    (22, 1, 0, "own", 0, 0, 1),
+    (22, 0, 0, "yline", 0, 2, 1),
+    (22, 0, 1, "xline", 0, 1, 1),
+    (22, 0, 0, "xline", 1, 3, 1),
+    (22, 0, 1, "yline", 1, 0, 1),
     (22, 1, 1, "own", 1, 0, 1),
-    (22, 1, 0, "yline", 0, 3, 1),
-    (22, 1, 0, "xline", 1, 0, 1),
     (22, 0, 1, "xline", 0, 0, 1),
-    (22, 0, 1, "own", 1, 2, 1),
     (22, 0, 1, "xline", 0, 2, 1),
     (22, 0, 0, "own", 0, 0, 1),
+    (22, 0, 0, "own", 0, 2, 1),
+    (22, 0, 0, "yline", 0, 3, 1),
     (22, 0, 1, "diag", 0, 3, 1),
-    (22, 0, 0, "yline", 0, 3, 1),
+    (22, 0, 1, "own", 1, 0, 1),
     (22, 0, 1, "xline", 0, 3, 1),
-    (22, 1, 0, "own", 0, 0, 1),
-    (22, 1, 0, "xline", 1, 2, 2),
+    (22, 1, 0, "xline", 1, 0, 1),
+    (22, 1, 1, "own", 1, 2, 1),
     (22, 1, 1, "xline", 0, 3, 1),
     (22, 1, 1, "yline", 1, 3, 1),
 )

time: 191 us -> 187 us (0.979)
  Pallas kernels: 188 us -> 183 us
    pallas_call x1, Pallas kernels: 98.3 us -> 92.2 us  [backward_scatter(): pl.pallas_call(functools.partial(backward_scatter_kernel, p), out_shape=[...]
where the time goes in v5:
time: 187 us; the launch traced here: 186 us
  Pallas kernels  183 us (98%)
    pallas_call x1, Pallas kernels, backward_scatter(): pl.pallas_call(functools.partial(backward_scatter_kernel, p), out_shape=[...  92.2 us
    pallas_call x1, Pallas kernels, gather_forward(): pl.pallas_call(functools.partial(gather_forward_kernel, p), out_shape=[S(...  86.9 us
    pallas_call x1, Pallas kernels, finish_copies(): pl.pallas_call(kernel, out_shape=[S((p.sh,), F32)] + [S(a.shape, a.dtype)...  3.93 us

profile of v5, /device:TPU:0, one launch (start us, length us, event | category | flops | bytes accessed | tf_op | source)
XLA Modules:
  0.0 186.1 jit_solution(11522253109255052216)
XLA Ops:
  1.3 1.8 pad_bitcast_fusion.x_ref
  3.1 86.9 %shard_map.84 = (bf16[512,768]{1,0:T(8,128)(2,1)}, f32[1,1728]{1,0:T(1,128)}, bf16[768,2304]{1,0:T(8,128)(2,1)}, bf16[768,768]{1,0:T(8,128)(2,1)}, bf16[768,3072...) custom-call(bf16[1731,128]{1,0:T(8,128)(2,1)} %pad_bitcast_fusion.x_, ...), custom_call_target="tpu_custom_call" | custom-call | tf_op jit(solution)/shard_map/pallas_call | solution.py:921
  90.0 92.2 %shard_map.85 = (f32[512,768]{1,0:T(8,128)}, f32[1731,128]{1,0:T(8,128)}) custom-call(s32[1]{0:T(128)S(6)} %copy.9.length, bf16[512,3072]{1,0:T(8,128)(2,1)} %get-tuple-element.28.refs_0_, bf16[512,768]{1,0:T(8,128)(2,1)} %get-tuple-element.29.refs_1_, bf16[3072,768]{1,0:T(8,128)(2,1)} %get-tuple-element.30.refs_2_, ...), custom_call_target="tpu_custom_call" | custom-call | tf_op jit(solution)/shard_map/pallas_call | solution.py:1238
  182.2 3.9 %shard_map.86 = (f32[221520]{0:T(1024)}, bf16[512,768]{1,0:T(8,128)(2,1)}, f32[512,768]{1,0:T(8,128)}, f32[1,1728]{1,0:T(1,128)}) custom-call(f32[1731,128]{1,0:T(8,128)} %get-tuple-element.44.a, bf16[512,768]{1,0:T(8,128)(2,1)} %get-tuple-element.45.b, f32[512,768]{1,0:T(8,128)} %get-tuple-element.46.c, f32[1,1728]{1,0:T(1,128)} %get-tuple-element.47.d), custom_call_target="tpu_custom_call" | custom-call | tf_op jit(solution)/shard_map/pallas_call | solution.py:1262

commit v6 on v5

--- a/solution.py
+++ b/solution.py
@@ -751,7 +751,12 @@
     r0 = r_first % 16
     lead = 32
     F[0 : lead + p.slot + 32] = jnp.zeros((lead + p.slot + 32, LN), F32)
-    F[lead : lead + p.rows_in] = pltpu.roll(x_ref[...].astype(F32), s, 1)
+    full = p.sh // LN
+    rest = p.sh - full * LN
+    F[lead : lead + full] = x_ref[: full * LN].astype(F32).reshape(full, LN)
+    if rest:
+        F[lead + full : lead + full + 1, :rest] = x_ref[full * LN :].astype(F32).reshape(1, rest)
+    F[lead : lead + p.rows_in] = pltpu.roll(F[lead : lead + p.rows_in], s, 1)
     lane = lax.broadcasted_iota(jnp.int32, (p.slot, LN), 1)
     G[me] = jnp.where(lane >= s, F[pl.ds(lead - r0, p.slot), :], F[pl.ds(lead - 1 - r0, p.slot), :]).astype(BF)
 
@@ -910,7 +915,6 @@
 
 
 def gather_forward(p, shard, length, tok, hcot, ncot):
-    x = jnp.pad(shard, (0, p.rows_in * LN - p.sh)).reshape(p.rows_in, LN)
     S = jax.ShapeDtypeStruct
     vm = pl.BlockSpec(memory_space=pltpu.VMEM)
     sm = pl.BlockSpec(memory_space=pltpu.SMEM)
@@ -927,7 +931,7 @@
         + [VM((p.n, p.slot, LN), BF), VM((6144 + 32, LN), F32), VM((1, 3 * D), F32), VM((LEN, D), F32), VM((LEN, 1), F32)]
         + [DM((p.n, 5)), DM((p.n, 2)), pltpu.SemaphoreType.REGULAR((2,)), DM((len(shapes),))],
         compiler_params=pltpu.CompilerParams(collective_id=0, has_side_effects=True, vmem_limit_bytes=64 << 20),
-    )(x, length, tok, hcot, ncot)
+    )(shard, length, tok, hcot, ncot)
     return dict(zip(FORWARD_OUT, res))
 
 

time: 187 us -> 186 us (level)
  no operation moved by 1% of the time
where the time goes in v6:
time: 186 us; the launch traced here: 185 us
  Pallas kernels  184 us (99%)
    pallas_call x1, Pallas kernels, backward_scatter(): pl.pallas_call(functools.partial(backward_scatter_kernel, p), out_shape=[...  92.2 us
    pallas_call x1, Pallas kernels, gather_forward(): pl.pallas_call(functools.partial(gather_forward_kernel, p), out_shape=[S(...  87.6 us
    pallas_call x1, Pallas kernels, finish_copies(): pl.pallas_call(kernel, out_shape=[S((p.sh,), F32)] + [S(a.shape, a.dtype)...  3.93 us

profile of v6, /device:TPU:0, one launch (start us, length us, event | category | flops | bytes accessed | tf_op | source)
XLA Modules:
  0.0 185.0 jit_solution(12984980787282277324)
XLA Ops:
  1.3 87.6 %shard_map.84 = (bf16[512,768]{1,0:T(8,128)(2,1)}, f32[1,1728]{1,0:T(1,128)}, bf16[768,2304]{1,0:T(8,128)(2,1)}, bf16[768,768]{1,0:T(8,128)(2,1)}, bf16[768,3072...) custom-call(bf16[221520]{0:T(1024)(128)(2,1)} %x_ref.1, ...), custom_call_target="tpu_custom_call" | custom-call | tf_op jit(solution)/shard_map/pallas_call | solution.py:925
  88.9 92.2 %shard_map.85 = (f32[512,768]{1,0:T(8,128)}, f32[1731,128]{1,0:T(8,128)}) custom-call(s32[1]{0:T(128)S(6)} %copy.9.length, bf16[512,3072]{1,0:T(8,128)(2,1)} %get-tuple-element.28.refs_0_, bf16[512,768]{1,0:T(8,128)(2,1)} %get-tuple-element.29.refs_1_, bf16[3072,768]{1,0:T(8,128)(2,1)} %get-tuple-element.30.refs_2_, ...), custom_call_target="tpu_custom_call" | custom-call | tf_op jit(solution)/shard_map/pallas_call | solution.py:1242
  181.1 3.9 %shard_map.86 = (f32[221520]{0:T(1024)}, bf16[512,768]{1,0:T(8,128)(2,1)}, f32[512,768]{1,0:T(8,128)}, f32[1,1728]{1,0:T(1,128)}) custom-call(f32[1731,128]{1,0:T(8,128)} %get-tuple-element.44.a, bf16[512,768]{1,0:T(8,128)(2,1)} %get-tuple-element.45.b, f32[512,768]{1,0:T(8,128)} %get-tuple-element.46.c, f32[1,1728]{1,0:T(1,128)} %get-tuple-element.47.d), custom_call_target="tpu_custom_call" | custom-call | tf_op jit(solution)/shard_map/pallas_call | solution.py:1266

commit v7 on v6

--- a/solution.py
+++ b/solution.py
@@ -519,7 +519,7 @@
         functools.partial(forward_kernel, p),
         out_shape=outs,
         in_specs=[vm, sm, vm, vm, vm],
-        scratch_shapes=[pltpu.VMEM((6144 + 32, LN), F32), pltpu.VMEM((1, 3 * D), F32), pltpu.VMEM((LEN, D), F32), pltpu.VMEM((LEN, 1), F32)],
+        scratch_shapes=[pltpu.VMEM((6144 + 64, LN), F32), pltpu.VMEM((1, 3 * D), F32), pltpu.VMEM((LEN, D), F32), pltpu.VMEM((LEN, 1), F32)],
         compiler_params=pltpu.CompilerParams(vmem_limit_bytes=60 << 20),
     )(slots, length, tok, hcot, ncot)
 
@@ -552,7 +552,7 @@
         functools.partial(backward_kernel, p),
         out_shape=[S((LEN, D), F32), S((flat_rows(p), LN), BF)],
         in_specs=[sm] + [vm] * 17,
-        scratch_shapes=[pltpu.VMEM((16, FF), F32), pltpu.VMEM((LEN, D), BF), pltpu.VMEM((LEN, D), BF), pltpu.VMEM((LEN, 3 * D), BF), pltpu.VMEM((6144 + 32, LN), F32), pltpu.VMEM((160, LN), F32)],
+        scratch_shapes=[pltpu.VMEM((16, FF), F32), pltpu.VMEM((LEN, D), BF), pltpu.VMEM((LEN, D), BF), pltpu.VMEM((LEN, 3 * D), BF), pltpu.VMEM((6144 + 64, LN), F32), pltpu.VMEM((160, LN), F32)],
         compiler_params=pltpu.CompilerParams(vmem_limit_bytes=60 << 20),
     )(length, tok, V, VG, qkv, lse, mixed, xh1, rstd1, first_low, act, gd, res, d_outer, wqkv, wo, w1, w2)
 
@@ -928,7 +928,7 @@
         in_specs=[vm, sm, vm, vm, vm],
         out_specs=[hbm] * len(shapes),
         scratch_shapes=[VM(*s) for s in shapes]
-        + [VM((p.n, p.slot, LN), BF), VM((6144 + 32, LN), F32), VM((1, 3 * D), F32), VM((LEN, D), F32), VM((LEN, 1), F32)]
+        + [VM((p.n, p.slot, LN), BF), VM((6144 + 64, LN), F32), VM((1, 3 * D), F32), VM((LEN, D), F32), VM((LEN, 1), F32)]
         + [DM((p.n, 5)), DM((p.n, 2)), pltpu.SemaphoreType.REGULAR((2,)), DM((len(shapes),))],
         compiler_params=pltpu.CompilerParams(collective_id=0, has_side_effects=True, vmem_limit_bytes=64 << 20),
     )(shard, length, tok, hcot, ncot)
@@ -1245,7 +1245,7 @@
         in_specs=[sm] + [hbm] * (len(ins) + 1),
         out_specs=[hbm, pl.BlockSpec(memory_space=pltpu.VMEM)],
         scratch_shapes=[VM(a.shape, a.dtype) for a in ins]
-        + [VM((flat_rows(p), LN), BF), VM((6144 + 32, LN), F32), VM((160, LN), F32), VM((16, SL, LN), BF), VM((4, half, LN), BF), VM((4, SL - half, LN), BF), VM((4, SL, LN), BF), VM((4, SL, LN), BF), VM((3, SL, LN), BF)]
+        + [VM((flat_rows(p), LN), BF), VM((6144 + 64, LN), F32), VM((160, LN), F32), VM((16, SL, LN), BF), VM((4, half, LN), BF), VM((4, SL - half, LN), BF), VM((4, SL, LN), BF), VM((4, SL, LN), BF), VM((3, SL, LN), BF)]
         + [DM((len(ins) + 3,)), DM, DM((16,)), DM((16,)), DM((2, 4)), DM((2, 4)), DM((4,)), DM((4,)), DM((4,)), DM((4,)), DM((3,)), DM((3,))],
         compiler_params=pltpu.CompilerParams(collective_id=1, has_side_effects=True, vmem_limit_bytes=64 << 20),
     )(length, *ins, wqkv)

time: 186 us -> 186 us (level)
  no operation moved by 1% of the time
where the time goes in v7:
time: 186 us; the launch traced here: 185 us
  Pallas kernels  184 us (99%)
    pallas_call x1, Pallas kernels, backward_scatter(): pl.pallas_call(functools.partial(backward_scatter_kernel, p), out_shape=[...  92.2 us
    pallas_call x1, Pallas kernels, gather_forward(): pl.pallas_call(functools.partial(gather_forward_kernel, p), out_shape=[S(...  87.6 us
    pallas_call x1, Pallas kernels, finish_copies(): pl.pallas_call(kernel, out_shape=[S((p.sh,), F32)] + [S(a.shape, a.dtype)...  3.93 us

profile of v7, /device:TPU:0, one launch (start us, length us, event | category | flops | bytes accessed | tf_op | source)
XLA Modules:
  0.0 185.0 jit_solution(9143828464462328555)
XLA Ops:
  1.3 87.6 %shard_map.84 = (bf16[512,768]{1,0:T(8,128)(2,1)}, f32[1,1728]{1,0:T(1,128)}, bf16[768,2304]{1,0:T(8,128)(2,1)}, bf16[768,768]{1,0:T(8,128)(2,1)}, bf16[768,3072...) custom-call(bf16[221520]{0:T(1024)(128)(2,1)} %x_ref.1, ...), custom_call_target="tpu_custom_call" | custom-call | tf_op jit(solution)/shard_map/pallas_call | solution.py:925
  88.9 92.2 %shard_map.85 = (f32[512,768]{1,0:T(8,128)}, f32[1731,128]{1,0:T(8,128)}) custom-call(s32[1]{0:T(128)S(6)} %copy.9.length, bf16[512,3072]{1,0:T(8,128)(2,1)} %get-tuple-element.28.refs_0_, bf16[512,768]{1,0:T(8,128)(2,1)} %get-tuple-element.29.refs_1_, bf16[3072,768]{1,0:T(8,128)(2,1)} %get-tuple-element.30.refs_2_, ...), custom_call_target="tpu_custom_call" | custom-call | tf_op jit(solution)/shard_map/pallas_call | solution.py:1242
  181.1 3.9 %shard_map.86 = (f32[221520]{0:T(1024)}, bf16[512,768]{1,0:T(8,128)(2,1)}, f32[512,768]{1,0:T(8,128)}, f32[1,1728]{1,0:T(1,128)}) custom-call(f32[1731,128]{1,0:T(8,128)} %get-tuple-element.44.a, bf16[512,768]{1,0:T(8,128)(2,1)} %get-tuple-element.45.b, f32[512,768]{1,0:T(8,128)} %get-tuple-element.46.c, f32[1,1728]{1,0:T(1,128)} %get-tuple-element.47.d), custom_call_target="tpu_custom_call" | custom-call | tf_op jit(solution)/shard_map/pallas_call | solution.py:1266

commit v8 on v7

--- a/solution.py
+++ b/solution.py
@@ -411,7 +411,7 @@
                 e = edge_at(base)
                 r.E[e : e + 16 - lead] = F[lead:16]
 
-        U = 256
+        U = 768
         to = base - lead + s * step_rows
 
         def emit(t, _):

time: 186 us -> 185 us (level)
  no operation moved by 1% of the time
where the time goes in v8:
time: 185 us
  Pallas kernels  183 us (99%)
    pallas_call x1, Pallas kernels, backward_scatter(): pl.pallas_call(functools.partial(backward_scatter_kernel, p), out_shape=[...  92 us
    pallas_call x1, Pallas kernels, gather_forward(): pl.pallas_call(functools.partial(gather_forward_kernel, p), out_shape=[S(...  87.6 us
    pallas_call x1, Pallas kernels, finish_copies(): pl.pallas_call(kernel, out_shape=[S((p.sh,), F32)] + [S(a.shape, a.dtype)...  3.93 us

profile of v8, /device:TPU:0, one launch (start us, length us, event | category | flops | bytes accessed | tf_op | source)
XLA Modules:
  0.0 184.8 jit_solution(12942518948977921001)
XLA Ops:
  1.3 87.6 %shard_map.84 = (bf16[512,768]{1,0:T(8,128)(2,1)}, f32[1,1728]{1,0:T(1,128)}, bf16[768,2304]{1,0:T(8,128)(2,1)}, bf16[768,768]{1,0:T(8,128)(2,1)}, bf16[768,3072...) custom-call(bf16[221520]{0:T(1024)(128)(2,1)} %x_ref.1, ...), custom_call_target="tpu_custom_call" | custom-call | tf_op jit(solution)/shard_map/pallas_call | solution.py:925
  88.9 92.0 %shard_map.85 = (f32[512,768]{1,0:T(8,128)}, f32[1731,128]{1,0:T(8,128)}) custom-call(s32[1]{0:T(128)S(6)} %copy.9.length, bf16[512,3072]{1,0:T(8,128)(2,1)} %get-tuple-element.28.refs_0_, bf16[512,768]{1,0:T(8,128)(2,1)} %get-tuple-element.29.refs_1_, bf16[3072,768]{1,0:T(8,128)(2,1)} %get-tuple-element.30.refs_2_, ...), custom_call_target="tpu_custom_call" | custom-call | tf_op jit(solution)/shard_map/pallas_call | solution.py:1242
  180.8 3.9 %shard_map.86 = (f32[221520]{0:T(1024)}, bf16[512,768]{1,0:T(8,128)(2,1)}, f32[512,768]{1,0:T(8,128)}, f32[1,1728]{1,0:T(1,128)}) custom-call(f32[1731,128]{1,0:T(8,128)} %get-tuple-element.44.a, bf16[512,768]{1,0:T(8,128)(2,1)} %get-tuple-element.45.b, f32[512,768]{1,0:T(8,128)} %get-tuple-element.46.c, f32[1,1728]{1,0:T(1,128)} %get-tuple-element.47.d), custom_call_target="tpu_custom_call" | custom-call | tf_op jit(solution)/shard_map/pallas_call | solution.py:1266
